TPU v7x, 128 devices: a whole 4x4x4 slice. The times are simulated.
128 devices in a mesh: sec: 8 (over x_lo, y), col: 16 (over x_hi, z, core).
Axes of the slice: x: 4 (x_hi: 2, x_lo: 2; x = x_hi * 2 + x_lo), y: 4, z: 4, core: 2. Of those that a mesh axis runs over, the one named last changes fastest.
Arguments:
- matrix_rows: float32 [8192, 32768], P('sec', 'col'), may hold values from -6 to 6
- factor_bank: float32 [4, 16, 512, 512], P(None, 'sec', 'col'), may hold values from -1 to 1, as said below
- owner_table: int32 [4, 16, 16], P(None, 'sec'), may hold values from 0 to 15, each once within a row
Outputs:
- updated: float32 [8192, 32768], P('sec', 'col')
Inputs may be any that keep to these rules, and one draw needn't show every extreme that they name: `factor_bank`: each factor G[r,k] is orthogonal. `owner_table`: for each round and section the list names every row block once.
All inputs are finite; a program needn't handle non-finite values.
Results may differ from a plain program's by a relative error of at most 0.00014.
Values sent between devices are 32-bit elements; how exact they have to be, the bound alone decides.
No kernel may reach another device: no remote copies, remote signals or barrier semaphores. Data moves between devices by JAX's collectives and lax.ppermute only.
A program may use at most 128 MiB of HBM per device.

v0:
```python
import jax
import jax.numpy as jnp
from jax import lax
from jax.experimental import pallas as pl
from jax.experimental.pallas import tpu as pltpu
from jax.sharding import PartitionSpec as P

F = 512
HALF = 256
TILE = 512
COST = 0.01
CHUNKS = ((0, 512), (512, 1024), (1536, 512))
VMEM = 16 * 1024 * 1024


def shifted(value, steps):
    count = lax.axis_size("sec")
    return lax.ppermute(value, "sec", [(i, (i + steps) % count) for i in range(count)])


def moved(value, target):
    return lax.ppermute(value, "col", [(i, target(i)) for i in range(16)])


def route(h, s):
    return lambda i: ((i // 8) ^ h) * 8 + ((i // 2 + s) % 4) * 2 + i % 2


STEPS = (0, 1, 3, 2)


def on_chip():
    return pl.BlockSpec(memory_space=pltpu.VMEM)


def kernel(body, args, in_specs, out_shapes, out_specs, flops, name, scratch=(), aliases=None):
    moved_bytes = sum(a.size * a.dtype.itemsize for a, b in zip(args, in_specs) if b.memory_space != pltpu.HBM)
    return pl.pallas_call(
        body,
        in_specs=in_specs,
        out_specs=out_specs,
        out_shape=out_shapes,
        scratch_shapes=scratch,
        input_output_aliases=aliases or {},
        compiler_params=pltpu.CompilerParams(vmem_limit_bytes=VMEM),
        cost_estimate=pl.CostEstimate(
            flops=int(COST * flops), bytes_accessed=int(COST * moved_bytes), transcendentals=0
        ),
        name=name,
    )(*args)


def prep(groups, index, owners, name, start=0):
    count = owners.shape[0]

    def body(owner_ref, *refs):
        ins, (hi_ref, lo_ref) = refs[: len(groups)], refs[len(groups) :]
        for array, at, source in index():
            for n in range(count):
                rows = pl.ds(pl.multiple_of(owner_ref[n, source] * 32, 32), 32)
                value = ins[array][at + (start + n,)]
                hi = value.astype(jnp.bfloat16)
                hi_ref[n, rows, :] = hi
                lo_ref[n, rows, :] = (value - hi.astype(jnp.float32)).astype(jnp.bfloat16)

    shape = jax.ShapeDtypeStruct((count, F, F), jnp.bfloat16)
    return kernel(
        body,
        (owners, *groups),
        [pl.BlockSpec(memory_space=pltpu.SMEM)] + [on_chip()] * len(groups),
        (shape, shape),
        (on_chip(), on_chip()),
        0,
        name,
    )


def placement():
    me = lax.axis_index("col")
    high, z, core = me // 8, (me // 2) % 4, me % 2
    out = []
    for q in (0, 1):
        for k, s in enumerate(STEPS):
            for h in (0, 1):
                x = high if h == 0 else 1 - high
                c = core if q == 0 else 1 - core
                out.append((4 * q + k, (h,), x * 8 + ((z + 4 - s) % 4) * 2 + c))
    return out


def spread(pair):
    return [pair] + [moved(pair, route(0, s)) for s in STEPS[1:]]


def both_cores(arrays):
    return arrays + [moved(a, lambda i: i ^ 1) for a in arrays]


def split(value):
    hi = value.astype(jnp.bfloat16)
    return hi, (value - hi.astype(jnp.float32)).astype(jnp.bfloat16)


def times(hi, lo, value):
    v_hi, v_lo = split(value)
    total = jnp.dot(hi, v_lo, preferred_element_type=jnp.float32)
    total += jnp.dot(lo, v_hi, preferred_element_type=jnp.float32)
    return total + jnp.dot(hi, v_hi, preferred_element_type=jnp.float32)


def work(windows, width):
    return windows * 3 * 2 * F * F * width


def strip_shapes(width):
    rows = (HALF, F, HALF)
    return tuple(jax.ShapeDtypeStruct((r, width), jnp.float32) for r in rows)


def tiles(width):
    return [slice(t, t + TILE) for t in range(0, width, TILE)]


def round0(strip, first, width, hi, lo):
    def body(x_ref, hi_ref, lo_ref, h0_ref, h12_ref, h3_ref, held, sems):
        copies = {}
        for t, part in enumerate(tiles(width)):
            for s in (0, 1):
                copies[t, s] = pltpu.make_async_copy(
                    x_ref.at[s * F : (s + 1) * F, first + part.start : first + part.stop],
                    held.at[t, s],
                    sems.at[t, s],
                )
                copies[t, s].start()
        for t, part in enumerate(tiles(width)):
            copies[t, 0].wait()
            s0 = times(hi_ref[0], lo_ref[0], held[t, 0])
            h0_ref[:, part] = s0[:HALF]
            h12_ref[:HALF, part] = s0[HALF:]
            copies[t, 1].wait()
            s1 = times(hi_ref[1], lo_ref[1], held[t, 1])
            h12_ref[HALF:, part] = s1[:HALF]
            h3_ref[:, part] = s1[HALF:]

    count = len(tiles(width))
    return kernel(
        body,
        (strip, hi, lo),
        [pl.BlockSpec(memory_space=pltpu.HBM), on_chip(), on_chip()],
        strip_shapes(width),
        (on_chip(),) * 3,
        work(2, width),
        "round0",
        [pltpu.VMEM((count, 2, F, TILE), jnp.float32), pltpu.SemaphoreType.DMA((count, 2))],
    )


def odd(above, h0, h12, h3, below, hi, lo):
    middle = times(hi[1], lo[1], h12)
    top = times(hi[0, HALF:, :HALF], lo[0, HALF:, :HALF], above)
    top += times(hi[0, HALF:, HALF:], lo[0, HALF:, HALF:], h0)
    bottom = times(hi[2, :HALF, :HALF], lo[2, :HALF, :HALF], h3)
    bottom += times(hi[2, :HALF, HALF:], lo[2, :HALF, HALF:], below)
    return top, middle, bottom


def rounds12(above, h0, h12, h3, below, hi, lo, outer=None):
    width = h0.shape[1]
    outer = outer or ()

    def body(a_ref, h0_ref, h12_ref, h3_ref, f_ref, hi_ref, lo_ref, *rest):
        o0, o12, o3 = rest[-3:]
        for part in tiles(width):
            a, f = a_ref[:, part], f_ref[:, part]
            if outer:
                out_hi, out_lo = rest[:2]
                a = times(out_hi[1, HALF:], out_lo[1, HALF:], a)
                f = times(out_hi[2, :HALF], out_lo[2, :HALF], f)
            top, middle, bottom = odd(
                a, h0_ref[:, part], h12_ref[:, part], h3_ref[:, part], f, hi_ref, lo_ref
            )
            s0 = times(hi_ref[3], lo_ref[3], jnp.concatenate([top, middle[:HALF]], 0))
            o0[:, part] = s0[:HALF]
            o12[:HALF, part] = s0[HALF:]
            s1 = times(hi_ref[4], lo_ref[4], jnp.concatenate([middle[HALF:], bottom], 0))
            o12[HALF:, part] = s1[:HALF]
            o3[:, part] = s1[HALF:]

    args = (above, h0, h12, h3, below, hi, lo, *outer)
    return kernel(
        body,
        args,
        [on_chip()] * len(args),
        strip_shapes(width),
        (on_chip(),) * 3,
        work(5 if outer else 4, width),
        "rounds12",
    )


def round3(above, h0, h12, h3, below, hi, lo, at, result, first, columns):
    width = h0.shape[1]

    def body(a_ref, h0_ref, h12_ref, h3_ref, f_ref, hi_ref, lo_ref, *rest):
        out, held, sems = rest[-3:]
        copies = []
        for t, part in enumerate(tiles(width)):
            parts = odd(
                a_ref[:, part],
                h0_ref[:, part],
                h12_ref[:, part],
                h3_ref[:, part],
                f_ref[:, part],
                hi_ref,
                lo_ref,
            )
            row = 0
            for p, value in enumerate(parts):
                rows = slice(row, row + value.shape[0])
                held[t, rows] = value
                copies.append(
                    pltpu.make_async_copy(
                        held.at[t, rows],
                        out.at[rows, first + part.start : first + part.stop],
                        sems.at[t, p],
                    )
                )
                copies[-1].start()
                row = rows.stop
        for copy in copies:
            copy.wait()

    args = [above, h0, h12, h3, below, hi, lo]
    specs = [on_chip()] * len(args)
    aliases = {}
    if result is not None:
        aliases = {len(args): 0}
        args.append(result)
        specs.append(pl.BlockSpec(memory_space=pltpu.HBM))
    count = len(tiles(width))
    return kernel(
        body,
        args,
        specs,
        jax.ShapeDtypeStruct((2 * F, columns), jnp.float32),
        pl.BlockSpec(memory_space=pltpu.HBM),
        work(2, width),
        "round3",
        [pltpu.VMEM((count, 2 * F, TILE), jnp.float32), pltpu.SemaphoreType.DMA((count, 3))],
        aliases,
    )


def exchanged(strip):
    h0, _, h3 = strip
    return shifted(h3, 1), shifted(h0, -1)


def after(value, *others):
    return lax.optimization_barrier((value, others))[0]


def local(matrix_rows, factor_bank, owner_table):
    columns = matrix_rows.shape[1]
    strip = pltpu.with_memory_space_constraint(matrix_rows, pltpu.HBM)
    beside = moved(factor_bank, route(1, 0))
    early = spread(jnp.stack([factor_bank[0], beside[0]]))
    places = jnp.pad(owner_table[:, 0].astype(jnp.float32), ((0, 4), (0, F - 16)))
    firsts = [bank[r, 0] for bank in (factor_bank, beside) for r in (1, 3)]
    following = shifted(jnp.concatenate(firsts + [places], 0), -1)
    next_owner = following[128:132, :16].astype(jnp.int32)
    following = following[:128].reshape(2, 2, 32, F)
    banks = tuple(zip((factor_bank, beside), following))
    mid = [jnp.concatenate([bank[1], new[:1], bank[2]], 0) for bank, new in banks]
    mid = spread(after(jnp.stack(mid), early[1]))
    late = [jnp.concatenate([bank[3], new[1:]], 0) for bank, new in banks]
    late = spread(after(jnp.stack(late), mid))

    hi0, lo0 = prep(both_cores(early), placement, owner_table[0], "place0")
    strips, halos = [], []
    for c, (first, width) in enumerate(CHUNKS):
        order = after(hi0, strips[-1][0]) if c else hi0
        order = after(order, halos[c - 2]) if c > 1 else order
        strips.append(round0(strip, first, width, order, lo0))
        halos.append(exchanged(strips[-1]))
    mid = both_cores(list(after(mid, strips[1], halos[0])))
    owners = jnp.concatenate([owner_table[1], next_owner[1:2], owner_table[2]], 0)
    hi12, lo12 = prep(mid, placement, owners, "place12")
    ready = list(halos)
    for c, (a, f) in enumerate(ready):
        order = after(hi12, strips[c - 1][0], ready[2]) if c else after(hi12, ready[1])
        order = after(order, halos[c - 2]) if c > 1 else order
        strips[c] = rounds12(a, *strips[c], f, order, lo12)
        halos[c] = exchanged(strips[c])
    late = both_cores(list(after(late, strips[1])))
    owners = jnp.concatenate([owner_table[3], next_owner[3:]], 0)
    hi3, lo3 = prep(late, placement, owners, "place3")
    result = None
    for (first, _), (h0, h12, h3), (a, f) in zip(CHUNKS, strips, halos):
        result = round3(a, h0, h12, h3, f, hi3, lo3, (0, 1, 2), result, first, columns)
    return result


def solution(mesh):
    in_specs = (P("sec", "col"), P(None, "sec", "col", None), P(None, "sec", None))
    out_specs = P("sec", "col")
    return jax.shard_map(local, mesh=mesh, in_specs=in_specs, out_specs=out_specs, check_vma=False)
```

profile of v0, /device:TPU:0, one launch (start us, length us, event | category | flops | bytes accessed | tf_op | source)
XLA Modules:
  0.0 157.6 jit_solution(15179111205141309284)
XLA Ops:
  0.0 3.1 %collective-permute-start = (f32[4,2,32,512]{3,2,1,0:T(8,128)}, f32[4,2,32,512]{3,2,1,0:T(8,128)S(1)}, u32[]{:S(2)}, u32[]{:S(2)}) collective-permute-start(f32[4,2,32,512]{3,2,1,0:T(8,128)} %param.4), channel_id=1, source_target_pairs={{0,8},{1,9},{2,10},{3,11},{4,12},{5,13},{6,14},{7,15},{8,0},{9,1},... | collective-permute-start | bytes 1572872 | tf_op jit(solution)/shard_map/ppermute | solution.py:22
  3.1 0.9 bitcast_dynamic-update-slice_fusion.1
  4.0 0.7 slice_convert_fusion.1
  4.7 0.8 bitcast_dynamic-update-slice_fusion
  5.5 1.1 slice_bitcast_fusion.3
  6.7 8.6 %collective-permute-done = f32[4,2,32,512]{3,2,1,0:T(8,128)S(1)} collective-permute-done((f32[4,2,32,512]{3,2,1,0:T(8,128)}, f32[4,2,32,512]{3,2,1,0:T(8,128)S(1)}, u32[]{:S(2)}, u32[]{:S(2)}) %collective-permute-start) | collective-permute-done | bytes 524320 | tf_op jit(solution)/shard_map/ppermute | solution.py:22
  15.3 4.2 %collective-permute-start.12 = (f32[136,512]{1,0:T(8,128)S(1)}, f32[136,512]{1,0:T(8,128)S(1)}, u32[]{:S(2)}, u32[]{:S(2)}) collective-permute-start(f32[136,512]{1,0:T(8,128)S(1)} %pad_dynamic-update-slice_fusion), channel_id=1, source_target_pairs={{0,112},{16,0},{32,16},{48,32},{64,48},{80,64},{96,80},{112,96},{1... | collective-permute-start | bytes 835592 | tf_op jit(solution)/shard_map/ppermute | solution.py:18
  19.6 4.0 %collective-permute-start.3 = (f32[2,2,32,512]{3,2,1,0:T(8,128)S(1)}, f32[2,2,32,512]{3,2,1,0:T(8,128)S(1)}, u32[]{:S(2)}, u32[]{:S(2)}) collective-permute-start(f32[2,2,32,512]{3,2,1,0:T(8,128)S(1)} %pad_maximum_fusion.2.refs_0_), channel_id=1, source_target_pairs={{0,4},{1,5},{2,6},{3,7},{4,0},{5,1},{6,2},{7,3},{8,12},{9,13},{10,... | collective-permute-start | bytes 786440 | tf_op jit(solution)/shard_map/ppermute | solution.py:22
  23.5 0.7 collective-permute-start.2
  24.2 1.3 collective-permute-start.1
  25.6 5.2 %collective-permute-done.3.refs_3_ = f32[2,2,32,512]{3,2,1,0:T(8,128)S(1)} collective-permute-done((f32[2,2,32,512]{3,2,1,0:T(8,128)S(1)}, f32[2,2,32,512]{3,2,1,0:T(8,128)S(1)}, u32[]{:S(2)}, u32[]{:S(2)}) %collective-permute-start.3) | collective-permute-done | bytes 262176 | tf_op jit(solution)/shard_map/ppermute | solution.py:22
  30.8 4.3 %collective-permute-done.2.refs_2_ = f32[2,2,32,512]{3,2,1,0:T(8,128)S(1)} collective-permute-done((f32[2,2,32,512]{3,2,1,0:T(8,128)S(1)}, f32[2,2,32,512]{3,2,1,0:T(8,128)S(1)}, u32[]{:S(2)}, u32[]{:S(2)}) %collective-permute-start.2) | collective-permute-done | bytes 262176 | tf_op jit(solution)/shard_map/ppermute | solution.py:22
  35.1 0.5 collective-permute-start.5
  35.7 2.0 %collective-permute-start.15 = (f32[2,5,32,512]{3,2,1,0:T(8,128)S(1)}, f32[2,5,32,512]{3,2,1,0:T(8,128)S(1)}, u32[]{:S(2)}, u32[]{:S(2)}) collective-permute-start(f32[2,5,32,512]{3,2,1,0:T(8,128)S(1)} %pad_maximum_fusion.refs_0_), channel_id=1, source_target_pairs={{0,4},{1,5},{2,6},{3,7},{4,0},{5,1},{6,2},{7,3},{8,12},{9,13},{10,... | collective-permute-start | bytes 1966088 | tf_op jit(solution)/shard_map/ppermute | solution.py:22
  37.8 1.2 collective-permute-start.14
  39.0 0.8 collective-permute-start.13
  39.8 0.9 place0.1
  40.7 3.2 %round0.3 = (f32[256,512]{1,0:T(8,128)S(1)}, f32[512,512]{1,0:T(8,128)S(1)}, f32[256,512]{1,0:T(8,128)S(1)}) custom-call(f32[1024,2048]{1,0:T(8,128)} %x_ref.5, bf16[2,512,512]{2,1,0:T(8,128)(2,1)S(1)} %get-tuple-element.53.hi_ref, bf16[2,512,512]{2,1,0:T(8,128)(2,1)S(1)} %get-tuple-element.47.lo_ref), custom_call_target="tpu_custom_call" | custom-call | flops 16106127 | bytes 20971 | tf_op jit(solution)/shard_map/round0/pallas_call | solution.py:38
  44.0 4.1 %collective-permute-start.9 = (f32[256,512]{1,0:T(8,128)S(1)}, f32[256,512]{1,0:T(8,128)S(1)}, u32[]{:S(2)}, u32[]{:S(2)}) collective-permute-start(f32[256,512]{1,0:T(8,128)S(1)} %get-tuple-element.48.h0_ref), channel_id=1, source_target_pairs={{0,112},{16,0},{32,16},{48,32},{64,48},{80,64},{96,80},{112,96},{1... | collective-permute-start | bytes 1572872 | tf_op jit(solution)/shard_map/ppermute | solution.py:18
  48.1 5.2 %round0.4 = (f32[256,1024]{1,0:T(8,128)S(1)}, f32[512,1024]{1,0:T(8,128)S(1)}, f32[256,1024]{1,0:T(8,128)S(1)}) custom-call(f32[1024,2048]{1,0:T(8,128)} %x_ref.5, bf16[2,512,512]{2,1,0:T(8,128)(2,1)S(1)} %get-tuple-element.53.hi_ref, bf16[2,512,512]{2,1,0:T(8,128)(2,1)S(1)} %get-tuple-element.47.lo_ref), custom_call_target="tpu_custom_call" | custom-call | flops 32212254 | bytes 20971 | tf_op jit(solution)/shard_map/round0/pallas_call | solution.py:38
  53.3 1.6 %collective-permute-done.15.refs_3_ = f32[2,5,32,512]{3,2,1,0:T(8,128)S(1)} collective-permute-done((f32[2,5,32,512]{3,2,1,0:T(8,128)S(1)}, f32[2,5,32,512]{3,2,1,0:T(8,128)S(1)}, u32[]{:S(2)}, u32[]{:S(2)}) %collective-permute-start.15) | collective-permute-done | bytes 655392 | tf_op jit(solution)/shard_map/ppermute | solution.py:22
  55.0 13.0 %collective-permute-done.14.refs_2_ = f32[2,5,32,512]{3,2,1,0:T(8,128)S(1)} collective-permute-done((f32[2,5,32,512]{3,2,1,0:T(8,128)S(1)}, f32[2,5,32,512]{3,2,1,0:T(8,128)S(1)}, u32[]{:S(2)}, u32[]{:S(2)}) %collective-permute-start.14) | collective-permute-done | bytes 655392 | tf_op jit(solution)/shard_map/ppermute | solution.py:22
  68.7 4.1 %collective-permute-start.21 = (f32[256,1024]{1,0:T(8,128)S(1)}, f32[256,1024]{1,0:T(8,128)S(1)}, u32[]{:S(2)}, u32[]{:S(2)}) collective-permute-start(f32[256,1024]{1,0:T(8,128)S(1)} %get-tuple-element.50.h0_ref), channel_id=1, source_target_pairs={{0,112},{16,0},{32,16},{48,32},{64,48},{80,64},{96,80},{112,96},{1... | collective-permute-start | bytes 3145736 | tf_op jit(solution)/shard_map/ppermute | solution.py:18
  72.8 3.2 %round0.5 = (f32[256,512]{1,0:T(8,128)S(1)}, f32[512,512]{1,0:T(8,128)S(1)}, f32[256,512]{1,0:T(8,128)S(1)}) custom-call(f32[1024,2048]{1,0:T(8,128)} %x_ref.5, bf16[2,512,512]{2,1,0:T(8,128)(2,1)S(1)} %get-tuple-element.53.hi_ref, bf16[2,512,512]{2,1,0:T(8,128)(2,1)S(1)} %get-tuple-element.47.lo_ref), custom_call_target="tpu_custom_call" | custom-call | flops 16106127 | bytes 20971 | tf_op jit(solution)/shard_map/round0/pallas_call | solution.py:38
  76.2 4.1 %collective-permute-start.11 = (f32[256,512]{1,0:T(8,128)S(1)}, f32[256,512]{1,0:T(8,128)S(1)}, u32[]{:S(2)}, u32[]{:S(2)}) collective-permute-start(f32[256,512]{1,0:T(8,128)S(1)} %get-tuple-element.55.h0_ref), channel_id=1, source_target_pairs={{0,112},{16,0},{32,16},{48,32},{64,48},{80,64},{96,80},{112,96},{1... | collective-permute-start | bytes 1572872 | tf_op jit(solution)/shard_map/ppermute | solution.py:18
  80.4 2.5 %collective-permute-start.28 = (f32[2,3,32,512]{3,2,1,0:T(8,128)S(1)}, f32[2,3,32,512]{3,2,1,0:T(8,128)S(1)}, u32[]{:S(2)}, u32[]{:S(2)}) collective-permute-start(f32[2,3,32,512]{3,2,1,0:T(8,128)S(1)} %pad_maximum_fusion.1.refs_0_), channel_id=1, source_target_pairs={{0,4},{1,5},{2,6},{3,7},{4,0},{5,1},{6,2},{7,3},{8,12},{9,13},{10,... | collective-permute-start | bytes 1179656 | tf_op jit(solution)/shard_map/ppermute | solution.py:22
  82.8 1.3 place12.1
  84.1 12.6 %collective-permute-done.20.a_ref = f32[256,1024]{1,0:T(8,128)S(1)} collective-permute-done((f32[256,1024]{1,0:T(8,128)S(1)}, f32[256,1024]{1,0:T(8,128)S(1)}, u32[]{:S(2)}, u32[]{:S(2)}) %collective-permute-start.20) | collective-permute-done | bytes 1048608 | tf_op jit(solution)/shard_map/ppermute | solution.py:18
  96.8 2.6 %collective-permute-start.27 = (f32[2,3,32,512]{3,2,1,0:T(8,128)S(1)}, f32[2,3,32,512]{3,2,1,0:T(8,128)S(1)}, u32[]{:S(2)}, u32[]{:S(2)}) collective-permute-start(f32[2,3,32,512]{3,2,1,0:T(8,128)S(1)} %pad_maximum_fusion.1.refs_0_), channel_id=1, source_target_pairs={{0,6},{1,7},{2,0},{3,1},{4,2},{5,3},{6,4},{7,5},{8,14},{9,15},{10,... | collective-permute-start | bytes 1179656 | tf_op jit(solution)/shard_map/ppermute | solution.py:22
  99.4 3.4 %rounds12.3 = (f32[256,512]{1,0:T(8,128)S(1)}, f32[512,512]{1,0:T(8,128)S(1)}, f32[256,512]{1,0:T(8,128)S(1)}) custom-call(f32[256,512]{1,0:T(8,128)S(1)} %collective-permute-done.8.a_ref, f32[256,512]{1,0:T(8,128)S(1)} %get-tuple-element.48.h0_ref, f32[512,512]{1,0:T(8,128)S(1)} %get-tuple-element.65.h12_ref, f32[256,512]{1,0:T(8,128)S(1)} %get-tuple-element.52.h3_ref, ...), custom_call_target="tpu_custom_call" | custom-call | flops 32212254 | bytes 83886 | tf_op jit(solution)/shard_map/rounds12/pallas_call | solution.py:38
  102.9 5.1 %collective-permute-done.10.a_ref = f32[256,512]{1,0:T(8,128)S(1)} collective-permute-done((f32[256,512]{1,0:T(8,128)S(1)}, f32[256,512]{1,0:T(8,128)S(1)}, u32[]{:S(2)}, u32[]{:S(2)}) %collective-permute-start.10) | collective-permute-done | bytes 524320 | tf_op jit(solution)/shard_map/ppermute | solution.py:18
  108.0 1.0 collective-permute-start.26
  109.0 6.7 %rounds12.4 = (f32[256,1024]{1,0:T(8,128)S(1)}, f32[512,1024]{1,0:T(8,128)S(1)}, f32[256,1024]{1,0:T(8,128)S(1)}) custom-call(f32[256,1024]{1,0:T(8,128)S(1)} %collective-permute-done.20.a_ref, f32[256,1024]{1,0:T(8,128)S(1)} %get-tuple-element.50.h0_ref, f32[512,1024]{1,0:T(8,128)S(1)} %get-tuple-element.58.h12_ref, ...), custom_call_target="tpu_custom_call" | custom-call | flops 64424508 | bytes 115343 | tf_op jit(solution)/shard_map/rounds12/pallas_call | solution.py:38
  115.7 2.1 %collective-permute-start.33 = (f32[256,1024]{1,0:T(8,128)S(1)}, f32[256,1024]{1,0:T(8,128)S(1)}, u32[]{:S(2)}, u32[]{:S(2)}) collective-permute-start(f32[256,1024]{1,0:T(8,128)S(1)} %get-tuple-element.79.h3_ref), channel_id=1, source_target_pairs={{0,16},{16,32},{32,48},{48,64},{64,80},{80,96},{96,112},{112,0},{1... | collective-permute-start | bytes 3145736 | tf_op jit(solution)/shard_map/ppermute | solution.py:18
  117.8 2.1 %collective-permute-start.34 = (f32[256,1024]{1,0:T(8,128)S(1)}, f32[256,1024]{1,0:T(8,128)S(1)}, u32[]{:S(2)}, u32[]{:S(2)}) collective-permute-start(f32[256,1024]{1,0:T(8,128)S(1)} %get-tuple-element.70.h0_ref), channel_id=1, source_target_pairs={{0,112},{16,0},{32,16},{48,32},{64,48},{80,64},{96,80},{112,96},{1... | collective-permute-start | bytes 3145736 | tf_op jit(solution)/shard_map/ppermute | solution.py:18
  119.9 0.5 collective-permute-start.30
  120.5 2.4 %collective-permute-done.23.f_ref = f32[256,512]{1,0:T(8,128)S(1)} collective-permute-done((f32[256,512]{1,0:T(8,128)S(1)}, f32[256,512]{1,0:T(8,128)S(1)}, u32[]{:S(2)}, u32[]{:S(2)}) %collective-permute-start.23) | collective-permute-done | bytes 524320 | tf_op jit(solution)/shard_map/ppermute | solution.py:18
  122.9 3.4 %rounds12.5 = (f32[256,512]{1,0:T(8,128)S(1)}, f32[512,512]{1,0:T(8,128)S(1)}, f32[256,512]{1,0:T(8,128)S(1)}) custom-call(f32[256,512]{1,0:T(8,128)S(1)} %collective-permute-done.10.a_ref, f32[256,512]{1,0:T(8,128)S(1)} %get-tuple-element.55.h0_ref, f32[512,512]{1,0:T(8,128)S(1)} %get-tuple-element.56.h12_ref, f32[256,512]{1,0:T(8,128)S(1)} %get-tuple-element.54.h3_ref, ...), custom_call_target="tpu_custom_call" | custom-call | flops 32212254 | bytes 83886 | tf_op jit(solution)/shard_map/rounds12/pallas_call | solution.py:38
  126.4 4.1 %collective-permute-start.25 = (f32[256,512]{1,0:T(8,128)S(1)}, f32[256,512]{1,0:T(8,128)S(1)}, u32[]{:S(2)}, u32[]{:S(2)}) collective-permute-start(f32[256,512]{1,0:T(8,128)S(1)} %get-tuple-element.75.h0_ref), channel_id=1, source_target_pairs={{0,112},{16,0},{32,16},{48,32},{64,48},{80,64},{96,80},{112,96},{1... | collective-permute-start | bytes 1572872 | tf_op jit(solution)/shard_map/ppermute | solution.py:18
  130.5 1.7 %collective-permute-done.32.refs_7_ = f32[2,3,32,512]{3,2,1,0:T(8,128)S(1)} collective-permute-done((f32[2,3,32,512]{3,2,1,0:T(8,128)S(1)}, f32[2,3,32,512]{3,2,1,0:T(8,128)S(1)}, u32[]{:S(2)}, u32[]{:S(2)}) %collective-permute-start.32) | collective-permute-done | bytes 393248 | tf_op jit(solution)/shard_map/ppermute | solution.py:22
  132.2 1.0 place3.1
  133.3 2.7 %round3.3.rest_0_ = f32[1024,2048]{1,0:T(8,128)} custom-call(f32[256,512]{1,0:T(8,128)S(1)} %collective-permute-done.22.a_ref, f32[256,512]{1,0:T(8,128)S(1)} %get-tuple-element.68.h0_ref, f32[512,512]{1,0:T(8,128)S(1)} %get-tuple-element.86.h12_ref, f32[256,512]{1,0:T(8,128)S(1)} %get-tuple-element.72.h3_ref, f32[256,512]{1,0:T(8,128)S(1)} %collective-permute-done.23.f_ref, ...), custom_call_target="tpu_custom_call" | custom-call | flops 16106127 | bytes 62914 | tf_op jit(solution)/shard_map/round3/pallas_call | solution.py:38
  136.0 8.0 %collective-permute-done.33.a_ref = f32[256,1024]{1,0:T(8,128)S(1)} collective-permute-done((f32[256,1024]{1,0:T(8,128)S(1)}, f32[256,1024]{1,0:T(8,128)S(1)}, u32[]{:S(2)}, u32[]{:S(2)}) %collective-permute-start.33) | collective-permute-done | bytes 1048608 | tf_op jit(solution)/shard_map/ppermute | solution.py:18
  144.0 1.3 collective-permute-done.34.f_ref
  145.3 4.5 %round3.4.rest_0_ = f32[1024,2048]{1,0:T(8,128)} custom-call(f32[256,1024]{1,0:T(8,128)S(1)} %collective-permute-done.33.a_ref, f32[256,1024]{1,0:T(8,128)S(1)} %get-tuple-element.70.h0_ref, f32[512,1024]{1,0:T(8,128)S(1)} %get-tuple-element.78.h12_ref, f32[256,1024]{1,0:T(8,128)S(1)} %get-tuple-element.79.h3_ref, ...), custom_call_target="tpu_custom_call", output_to_operand_aliasing={{}: (7, {})} | custom-call | flops 32212254 | bytes 94371 | tf_op jit(solution)/shard_map/round3/pallas_call | solution.py:38
  149.8 3.3 %collective-permute-done.24.a_ref = f32[256,512]{1,0:T(8,128)S(1)} collective-permute-done((f32[256,512]{1,0:T(8,128)S(1)}, f32[256,512]{1,0:T(8,128)S(1)}, u32[]{:S(2)}, u32[]{:S(2)}) %collective-permute-start.24) | collective-permute-done | bytes 524320 | tf_op jit(solution)/shard_map/ppermute | solution.py:18
  153.1 1.6 %collective-permute-done.25.f_ref = f32[256,512]{1,0:T(8,128)S(1)} collective-permute-done((f32[256,512]{1,0:T(8,128)S(1)}, f32[256,512]{1,0:T(8,128)S(1)}, u32[]{:S(2)}, u32[]{:S(2)}) %collective-permute-start.25) | collective-permute-done | bytes 524320 | tf_op jit(solution)/shard_map/ppermute | solution.py:18
  154.7 2.7 %round3.5 = f32[1024,2048]{1,0:T(8,128)} custom-call(f32[256,512]{1,0:T(8,128)S(1)} %collective-permute-done.24.a_ref, f32[256,512]{1,0:T(8,128)S(1)} %get-tuple-element.75.h0_ref, f32[512,512]{1,0:T(8,128)S(1)} %get-tuple-element.76.h12_ref, f32[256,512]{1,0:T(8,128)S(1)} %get-tuple-element.74.h3_ref, ...), custom_call_target="tpu_custom_call", output_to_operand_aliasing={{}: (7, {})} | custom-call | flops 16106127 | bytes 62914 | tf_op jit(solution)/shard_map/round3/pallas_call | solution.py:38
  (55 shorter events, 1.4 us)
Async XLA Ops:
  0.0 15.2 %collective-permute-start = (f32[4,2,32,512]{3,2,1,0:T(8,128)}, f32[4,2,32,512]{3,2,1,0:T(8,128)S(1)}, u32[]{:S(2)}, u32[]{:S(2)}) collective-permute-start(f32[4,2,32,512]{3,2,1,0:T(8,128)} %param.4), channel_id=1, source_target_pairs={{0,8},{1,9},{2,10},{3,11},{4,12},{5,13},{6,14},{7,15},{8,0},{9,1},... | collective-permute-start | bytes 1572872 | tf_op jit(solution)/shard_map/ppermute | solution.py:22
  6.7 33.2 %copy-start = (s32[4,2,16]{2,1,0:T(2,128)S(1)}, s32[4,2,16]{2,1,0:T(2,128)}, u32[]{:S(2)}) copy-start(s32[4,2,16]{2,1,0:T(2,128)} %param.5) | copy-start | bytes 1540
  15.3 20.3 %collective-permute-start.12 = (f32[136,512]{1,0:T(8,128)S(1)}, f32[136,512]{1,0:T(8,128)S(1)}, u32[]{:S(2)}, u32[]{:S(2)}) collective-permute-start(f32[136,512]{1,0:T(8,128)S(1)} %pad_dynamic-update-slice_fusion), channel_id=1, source_target_pairs={{0,112},{16,0},{32,16},{48,32},{64,48},{80,64},{96,80},{112,96},{1... | collective-permute-start | bytes 835592 | tf_op jit(solution)/shard_map/ppermute | solution.py:18
  19.6 11.2 %collective-permute-start.3 = (f32[2,2,32,512]{3,2,1,0:T(8,128)S(1)}, f32[2,2,32,512]{3,2,1,0:T(8,128)S(1)}, u32[]{:S(2)}, u32[]{:S(2)}) collective-permute-start(f32[2,2,32,512]{3,2,1,0:T(8,128)S(1)} %pad_maximum_fusion.2.refs_0_), channel_id=1, source_target_pairs={{0,4},{1,5},{2,6},{3,7},{4,0},{5,1},{6,2},{7,3},{8,12},{9,13},{10,... | collective-permute-start | bytes 786440 | tf_op jit(solution)/shard_map/ppermute | solution.py:22
  23.5 11.5 %collective-permute-start.2 = (f32[2,2,32,512]{3,2,1,0:T(8,128)S(1)}, f32[2,2,32,512]{3,2,1,0:T(8,128)S(1)}, u32[]{:S(2)}, u32[]{:S(2)}) collective-permute-start(f32[2,2,32,512]{3,2,1,0:T(8,128)S(1)} %pad_maximum_fusion.2.refs_0_), channel_id=1, source_target_pairs={{0,6},{1,7},{2,0},{3,1},{4,2},{5,3},{6,4},{7,5},{8,14},{9,15},{10,... | collective-permute-start | bytes 786440 | tf_op jit(solution)/shard_map/ppermute | solution.py:22
  24.2 10.8 %collective-permute-start.1 = (f32[2,2,32,512]{3,2,1,0:T(8,128)S(1)}, f32[2,2,32,512]{3,2,1,0:T(8,128)S(1)}, u32[]{:S(2)}, u32[]{:S(2)}) collective-permute-start(f32[2,2,32,512]{3,2,1,0:T(8,128)S(1)} %pad_maximum_fusion.2.refs_0_), channel_id=1, source_target_pairs={{0,2},{1,3},{2,4},{3,5},{4,6},{5,7},{6,0},{7,1},{8,10},{9,11},{10,... | collective-permute-start | bytes 786440 | tf_op jit(solution)/shard_map/ppermute | solution.py:22
  25.6 12.2 %collective-permute-start.4 = (f32[2,2,32,512]{3,2,1,0:T(8,128)S(1)}, f32[2,2,32,512]{3,2,1,0:T(8,128)S(1)}, u32[]{:S(2)}, u32[]{:S(2)}) collective-permute-start(f32[2,2,32,512]{3,2,1,0:T(8,128)S(1)} %pad_maximum_fusion.2.refs_0_), channel_id=1, source_target_pairs={{0,1},{1,0},{2,3},{3,2},{4,5},{5,4},{6,7},{7,6},{8,9},{9,8},{10,11... | collective-permute-start | bytes 786440 | tf_op jit(solution)/shard_map/ppermute | solution.py:22
  30.8 8.2 %collective-permute-start.7 = (f32[2,2,32,512]{3,2,1,0:T(8,128)S(1)}, f32[2,2,32,512]{3,2,1,0:T(8,128)S(1)}, u32[]{:S(2)}, u32[]{:S(2)}) collective-permute-start(f32[2,2,32,512]{3,2,1,0:T(8,128)S(1)} %collective-permute-done.3.refs_3_), channel_id=1, source_target_pairs={{0,1},{1,0},{2,3},{3,2},{4,5},{5,4},{6,7},{7,6},{8,9},{9,8},{10,11... | collective-permute-start | bytes 786440 | tf_op jit(solution)/shard_map/ppermute | solution.py:22
  35.1 4.7 %collective-permute-start.6 = (f32[2,2,32,512]{3,2,1,0:T(8,128)S(1)}, f32[2,2,32,512]{3,2,1,0:T(8,128)S(1)}, u32[]{:S(2)}, u32[]{:S(2)}) collective-permute-start(f32[2,2,32,512]{3,2,1,0:T(8,128)S(1)} %collective-permute-done.2.refs_2_), channel_id=1, source_target_pairs={{0,1},{1,0},{2,3},{3,2},{4,5},{5,4},{6,7},{7,6},{8,9},{9,8},{10,11... | collective-permute-start | bytes 786440 | tf_op jit(solution)/shard_map/ppermute | solution.py:22
  35.1 4.7 %collective-permute-start.5 = (f32[2,2,32,512]{3,2,1,0:T(8,128)S(1)}, f32[2,2,32,512]{3,2,1,0:T(8,128)S(1)}, u32[]{:S(2)}, u32[]{:S(2)}) collective-permute-start(f32[2,2,32,512]{3,2,1,0:T(8,128)S(1)} %collective-permute-done.1.refs_1_), channel_id=1, source_target_pairs={{0,1},{1,0},{2,3},{3,2},{4,5},{5,4},{6,7},{7,6},{8,9},{9,8},{10,11... | collective-permute-start | bytes 786440 | tf_op jit(solution)/shard_map/ppermute | solution.py:22
  35.7 19.2 %collective-permute-start.15 = (f32[2,5,32,512]{3,2,1,0:T(8,128)S(1)}, f32[2,5,32,512]{3,2,1,0:T(8,128)S(1)}, u32[]{:S(2)}, u32[]{:S(2)}) collective-permute-start(f32[2,5,32,512]{3,2,1,0:T(8,128)S(1)} %pad_maximum_fusion.refs_0_), channel_id=1, source_target_pairs={{0,4},{1,5},{2,6},{3,7},{4,0},{5,1},{6,2},{7,3},{8,12},{9,13},{10,... | collective-permute-start | bytes 1966088 | tf_op jit(solution)/shard_map/ppermute | solution.py:22
  37.8 30.2 %collective-permute-start.14 = (f32[2,5,32,512]{3,2,1,0:T(8,128)S(1)}, f32[2,5,32,512]{3,2,1,0:T(8,128)S(1)}, u32[]{:S(2)}, u32[]{:S(2)}) collective-permute-start(f32[2,5,32,512]{3,2,1,0:T(8,128)S(1)} %pad_maximum_fusion.refs_0_), channel_id=1, source_target_pairs={{0,6},{1,7},{2,0},{3,1},{4,2},{5,3},{6,4},{7,5},{8,14},{9,15},{10,... | collective-permute-start | bytes 1966088 | tf_op jit(solution)/shard_map/ppermute | solution.py:22
  39.0 29.0 %collective-permute-start.13 = (f32[2,5,32,512]{3,2,1,0:T(8,128)S(1)}, f32[2,5,32,512]{3,2,1,0:T(8,128)S(1)}, u32[]{:S(2)}, u32[]{:S(2)}) collective-permute-start(f32[2,5,32,512]{3,2,1,0:T(8,128)S(1)} %pad_maximum_fusion.refs_0_), channel_id=1, source_target_pairs={{0,2},{1,3},{2,4},{3,5},{4,6},{5,7},{6,0},{7,1},{8,10},{9,11},{10,... | collective-permute-start | bytes 1966088 | tf_op jit(solution)/shard_map/ppermute | solution.py:22
  43.9 24.1 %collective-permute-start.8 = (f32[256,512]{1,0:T(8,128)S(1)}, f32[256,512]{1,0:T(8,128)S(1)}, u32[]{:S(2)}, u32[]{:S(2)}) collective-permute-start(f32[256,512]{1,0:T(8,128)S(1)} %get-tuple-element.52.h3_ref), channel_id=1, source_target_pairs={{0,16},{16,32},{32,48},{48,64},{64,80},{80,96},{96,112},{112,0},{1... | collective-permute-start | bytes 1572872 | tf_op jit(solution)/shard_map/ppermute | solution.py:18
  44.0 24.0 %collective-permute-start.9 = (f32[256,512]{1,0:T(8,128)S(1)}, f32[256,512]{1,0:T(8,128)S(1)}, u32[]{:S(2)}, u32[]{:S(2)}) collective-permute-start(f32[256,512]{1,0:T(8,128)S(1)} %get-tuple-element.48.h0_ref), channel_id=1, source_target_pairs={{0,112},{16,0},{32,16},{48,32},{64,48},{80,64},{96,80},{112,96},{1... | collective-permute-start | bytes 1572872 | tf_op jit(solution)/shard_map/ppermute | solution.py:18
  68.0 4.8 %collective-permute-start.16 = (f32[2,5,32,512]{3,2,1,0:T(8,128)S(1)}, f32[2,5,32,512]{3,2,1,0:T(8,128)S(1)}, u32[]{:S(2)}, u32[]{:S(2)}) collective-permute-start(f32[2,5,32,512]{3,2,1,0:T(8,128)S(1)} %pad_maximum_fusion.refs_0_), channel_id=1, source_target_pairs={{0,1},{1,0},{2,3},{3,2},{4,5},{5,4},{6,7},{7,6},{8,9},{9,8},{10,11... | collective-permute-start | bytes 1966088 | tf_op jit(solution)/shard_map/ppermute | solution.py:22
  68.1 8.0 %collective-permute-start.17 = (f32[2,5,32,512]{3,2,1,0:T(8,128)S(1)}, f32[2,5,32,512]{3,2,1,0:T(8,128)S(1)}, u32[]{:S(2)}, u32[]{:S(2)}) collective-permute-start(f32[2,5,32,512]{3,2,1,0:T(8,128)S(1)} %collective-permute-done.13.refs_1_), channel_id=1, source_target_pairs={{0,1},{1,0},{2,3},{3,2},{4,5},{5,4},{6,7},{7,6},{8,9},{9,8},{10,11... | collective-permute-start | bytes 1966088 | tf_op jit(solution)/shard_map/ppermute | solution.py:22
  68.6 7.6 %collective-permute-start.18 = (f32[2,5,32,512]{3,2,1,0:T(8,128)S(1)}, f32[2,5,32,512]{3,2,1,0:T(8,128)S(1)}, u32[]{:S(2)}, u32[]{:S(2)}) collective-permute-start(f32[2,5,32,512]{3,2,1,0:T(8,128)S(1)} %collective-permute-done.14.refs_2_), channel_id=1, source_target_pairs={{0,1},{1,0},{2,3},{3,2},{4,5},{5,4},{6,7},{7,6},{8,9},{9,8},{10,11... | collective-permute-start | bytes 1966088 | tf_op jit(solution)/shard_map/ppermute | solution.py:22
  68.7 28.1 %collective-permute-start.20 = (f32[256,1024]{1,0:T(8,128)S(1)}, f32[256,1024]{1,0:T(8,128)S(1)}, u32[]{:S(2)}, u32[]{:S(2)}) collective-permute-start(f32[256,1024]{1,0:T(8,128)S(1)} %get-tuple-element.59.h3_ref), channel_id=1, source_target_pairs={{0,16},{16,32},{32,48},{48,64},{64,80},{80,96},{96,112},{112,0},{1... | collective-permute-start | bytes 3145736 | tf_op jit(solution)/shard_map/ppermute | solution.py:18
  68.7 30.7 %collective-permute-start.21 = (f32[256,1024]{1,0:T(8,128)S(1)}, f32[256,1024]{1,0:T(8,128)S(1)}, u32[]{:S(2)}, u32[]{:S(2)}) collective-permute-start(f32[256,1024]{1,0:T(8,128)S(1)} %get-tuple-element.50.h0_ref), channel_id=1, source_target_pairs={{0,112},{16,0},{32,16},{48,32},{64,48},{80,64},{96,80},{112,96},{1... | collective-permute-start | bytes 3145736 | tf_op jit(solution)/shard_map/ppermute | solution.py:18
  72.8 7.5 %collective-permute-start.19 = (f32[2,5,32,512]{3,2,1,0:T(8,128)S(1)}, f32[2,5,32,512]{3,2,1,0:T(8,128)S(1)}, u32[]{:S(2)}, u32[]{:S(2)}) collective-permute-start(f32[2,5,32,512]{3,2,1,0:T(8,128)S(1)} %collective-permute-done.15.refs_3_), channel_id=1, source_target_pairs={{0,1},{1,0},{2,3},{3,2},{4,5},{5,4},{6,7},{7,6},{8,9},{9,8},{10,11... | collective-permute-start | bytes 1966088 | tf_op jit(solution)/shard_map/ppermute | solution.py:22
  76.1 31.9 %collective-permute-start.10 = (f32[256,512]{1,0:T(8,128)S(1)}, f32[256,512]{1,0:T(8,128)S(1)}, u32[]{:S(2)}, u32[]{:S(2)}) collective-permute-start(f32[256,512]{1,0:T(8,128)S(1)} %get-tuple-element.54.h3_ref), channel_id=1, source_target_pairs={{0,16},{16,32},{32,48},{48,64},{64,80},{80,96},{96,112},{112,0},{1... | collective-permute-start | bytes 1572872 | tf_op jit(solution)/shard_map/ppermute | solution.py:18
  76.2 31.9 %collective-permute-start.11 = (f32[256,512]{1,0:T(8,128)S(1)}, f32[256,512]{1,0:T(8,128)S(1)}, u32[]{:S(2)}, u32[]{:S(2)}) collective-permute-start(f32[256,512]{1,0:T(8,128)S(1)} %get-tuple-element.55.h0_ref), channel_id=1, source_target_pairs={{0,112},{16,0},{32,16},{48,32},{64,48},{80,64},{96,80},{112,96},{1... | collective-permute-start | bytes 1572872 | tf_op jit(solution)/shard_map/ppermute | solution.py:18
  80.4 35.3 %collective-permute-start.28 = (f32[2,3,32,512]{3,2,1,0:T(8,128)S(1)}, f32[2,3,32,512]{3,2,1,0:T(8,128)S(1)}, u32[]{:S(2)}, u32[]{:S(2)}) collective-permute-start(f32[2,3,32,512]{3,2,1,0:T(8,128)S(1)} %pad_maximum_fusion.1.refs_0_), channel_id=1, source_target_pairs={{0,4},{1,5},{2,6},{3,7},{4,0},{5,1},{6,2},{7,3},{8,12},{9,13},{10,... | collective-permute-start | bytes 1179656 | tf_op jit(solution)/shard_map/ppermute | solution.py:22
  96.8 21.1 %collective-permute-start.27 = (f32[2,3,32,512]{3,2,1,0:T(8,128)S(1)}, f32[2,3,32,512]{3,2,1,0:T(8,128)S(1)}, u32[]{:S(2)}, u32[]{:S(2)}) collective-permute-start(f32[2,3,32,512]{3,2,1,0:T(8,128)S(1)} %pad_maximum_fusion.1.refs_0_), channel_id=1, source_target_pairs={{0,6},{1,7},{2,0},{3,1},{4,2},{5,3},{6,4},{7,5},{8,14},{9,15},{10,... | collective-permute-start | bytes 1179656 | tf_op jit(solution)/shard_map/ppermute | solution.py:22
  102.8 17.1 %collective-permute-start.22 = (f32[256,512]{1,0:T(8,128)S(1)}, f32[256,512]{1,0:T(8,128)S(1)}, u32[]{:S(2)}, u32[]{:S(2)}) collective-permute-start(f32[256,512]{1,0:T(8,128)S(1)} %get-tuple-element.72.h3_ref), channel_id=1, source_target_pairs={{0,16},{16,32},{32,48},{48,64},{64,80},{80,96},{96,112},{112,0},{1... | collective-permute-start | bytes 1572872 | tf_op jit(solution)/shard_map/ppermute | solution.py:18
  108.0 14.9 %collective-permute-start.23 = (f32[256,512]{1,0:T(8,128)S(1)}, f32[256,512]{1,0:T(8,128)S(1)}, u32[]{:S(2)}, u32[]{:S(2)}) collective-permute-start(f32[256,512]{1,0:T(8,128)S(1)} %get-tuple-element.68.h0_ref), channel_id=1, source_target_pairs={{0,112},{16,0},{32,16},{48,32},{64,48},{80,64},{96,80},{112,96},{1... | collective-permute-start | bytes 1572872 | tf_op jit(solution)/shard_map/ppermute | solution.py:18
  108.0 11.9 %collective-permute-start.26 = (f32[2,3,32,512]{3,2,1,0:T(8,128)S(1)}, f32[2,3,32,512]{3,2,1,0:T(8,128)S(1)}, u32[]{:S(2)}, u32[]{:S(2)}) collective-permute-start(f32[2,3,32,512]{3,2,1,0:T(8,128)S(1)} %pad_maximum_fusion.1.refs_0_), channel_id=1, source_target_pairs={{0,2},{1,3},{2,4},{3,5},{4,6},{5,7},{6,0},{7,1},{8,10},{9,11},{10,... | collective-permute-start | bytes 1179656 | tf_op jit(solution)/shard_map/ppermute | solution.py:22
  115.7 28.3 %collective-permute-start.33 = (f32[256,1024]{1,0:T(8,128)S(1)}, f32[256,1024]{1,0:T(8,128)S(1)}, u32[]{:S(2)}, u32[]{:S(2)}) collective-permute-start(f32[256,1024]{1,0:T(8,128)S(1)} %get-tuple-element.79.h3_ref), channel_id=1, source_target_pairs={{0,16},{16,32},{32,48},{48,64},{64,80},{80,96},{96,112},{112,0},{1... | collective-permute-start | bytes 3145736 | tf_op jit(solution)/shard_map/ppermute | solution.py:18
  117.8 27.5 %collective-permute-start.34 = (f32[256,1024]{1,0:T(8,128)S(1)}, f32[256,1024]{1,0:T(8,128)S(1)}, u32[]{:S(2)}, u32[]{:S(2)}) collective-permute-start(f32[256,1024]{1,0:T(8,128)S(1)} %get-tuple-element.70.h0_ref), channel_id=1, source_target_pairs={{0,112},{16,0},{32,16},{48,32},{64,48},{80,64},{96,80},{112,96},{1... | collective-permute-start | bytes 3145736 | tf_op jit(solution)/shard_map/ppermute | solution.py:18
  119.9 6.4 %collective-permute-start.29 = (f32[2,3,32,512]{3,2,1,0:T(8,128)S(1)}, f32[2,3,32,512]{3,2,1,0:T(8,128)S(1)}, u32[]{:S(2)}, u32[]{:S(2)}) collective-permute-start(f32[2,3,32,512]{3,2,1,0:T(8,128)S(1)} %pad_maximum_fusion.1.refs_0_), channel_id=1, source_target_pairs={{0,1},{1,0},{2,3},{3,2},{4,5},{5,4},{6,7},{7,6},{8,9},{9,8},{10,11... | collective-permute-start | bytes 1179656 | tf_op jit(solution)/shard_map/ppermute | solution.py:22
  119.9 6.4 %collective-permute-start.30 = (f32[2,3,32,512]{3,2,1,0:T(8,128)S(1)}, f32[2,3,32,512]{3,2,1,0:T(8,128)S(1)}, u32[]{:S(2)}, u32[]{:S(2)}) collective-permute-start(f32[2,3,32,512]{3,2,1,0:T(8,128)S(1)} %collective-permute-done.26.refs_1_), channel_id=1, source_target_pairs={{0,1},{1,0},{2,3},{3,2},{4,5},{5,4},{6,7},{7,6},{8,9},{9,8},{10,11... | collective-permute-start | bytes 1179656 | tf_op jit(solution)/shard_map/ppermute | solution.py:22
  122.9 7.7 %collective-permute-start.31 = (f32[2,3,32,512]{3,2,1,0:T(8,128)S(1)}, f32[2,3,32,512]{3,2,1,0:T(8,128)S(1)}, u32[]{:S(2)}, u32[]{:S(2)}) collective-permute-start(f32[2,3,32,512]{3,2,1,0:T(8,128)S(1)} %collective-permute-done.27.refs_2_), channel_id=1, source_target_pairs={{0,1},{1,0},{2,3},{3,2},{4,5},{5,4},{6,7},{7,6},{8,9},{9,8},{10,11... | collective-permute-start | bytes 1179656 | tf_op jit(solution)/shard_map/ppermute | solution.py:22
  126.3 26.8 %collective-permute-start.24 = (f32[256,512]{1,0:T(8,128)S(1)}, f32[256,512]{1,0:T(8,128)S(1)}, u32[]{:S(2)}, u32[]{:S(2)}) collective-permute-start(f32[256,512]{1,0:T(8,128)S(1)} %get-tuple-element.74.h3_ref), channel_id=1, source_target_pairs={{0,16},{16,32},{32,48},{48,64},{64,80},{80,96},{96,112},{112,0},{1... | collective-permute-start | bytes 1572872 | tf_op jit(solution)/shard_map/ppermute | solution.py:18
  126.4 28.3 %collective-permute-start.25 = (f32[256,512]{1,0:T(8,128)S(1)}, f32[256,512]{1,0:T(8,128)S(1)}, u32[]{:S(2)}, u32[]{:S(2)}) collective-permute-start(f32[256,512]{1,0:T(8,128)S(1)} %get-tuple-element.75.h0_ref), channel_id=1, source_target_pairs={{0,112},{16,0},{32,16},{48,32},{64,48},{80,64},{96,80},{112,96},{1... | collective-permute-start | bytes 1572872 | tf_op jit(solution)/shard_map/ppermute | solution.py:18
  130.5 1.7 %collective-permute-start.32 = (f32[2,3,32,512]{3,2,1,0:T(8,128)S(1)}, f32[2,3,32,512]{3,2,1,0:T(8,128)S(1)}, u32[]{:S(2)}, u32[]{:S(2)}) collective-permute-start(f32[2,3,32,512]{3,2,1,0:T(8,128)S(1)} %collective-permute-done.28.refs_3_), channel_id=1, source_target_pairs={{0,1},{1,0},{2,3},{3,2},{4,5},{5,4},{6,7},{7,6},{8,9},{9,8},{10,11... | collective-permute-start | bytes 1179656 | tf_op jit(solution)/shard_map/ppermute | solution.py:22
where the time goes:
time: 158 us
  waiting for transfers between devices  68.9 us (44%)
  starting transfers between devices  46.2 us (29%)
  Pallas kernels  38.2 us (24%)
  local copies, waits for them, and re-layouts  2.94 us (2%)
    pallas_call x12, Pallas kernels, kernel(): pl.pallas_call(body, in_specs=in_specs, out_specs=out_specs, out_shape=ou...  38.2 us
    ppermute x22, waiting for transfers between devices, moved(): return lax.ppermute(value, 'col', [(i, target(i)) for i in range(16)])  34.5 us
    ppermute x13, waiting for transfers between devices, shifted(): lax.ppermute(value, 'sec', [(i, (i + steps) % count) for i in range(count)])  34.4 us
    ppermute x13, starting transfers between devices, shifted(): lax.ppermute(value, 'sec', [(i, (i + steps) % count) for i in range(count)])  25.2 us
    ppermute x22, starting transfers between devices, moved(): return lax.ppermute(value, 'col', [(i, target(i)) for i in range(16)])  20.9 us
  transfers between devices with their start and end apart: 35, of which 13 were waited for; matrix products, arithmetic and copies ran while one was open for 2% of the time, Pallas kernels for 23%

commit v1 on v0

--- a/solution.py
+++ b/solution.py
@@ -9,7 +9,7 @@
 HALF = 256
 TILE = 512
 COST = 0.01
-CHUNKS = ((0, 512), (512, 1024), (1536, 512))
+CHUNKS = ((0, 1024), (1024, 512), (1536, 512))
 VMEM = 16 * 1024 * 1024
 
 
@@ -263,18 +263,17 @@
 def local(matrix_rows, factor_bank, owner_table):
     columns = matrix_rows.shape[1]
     strip = pltpu.with_memory_space_constraint(matrix_rows, pltpu.HBM)
-    beside = moved(factor_bank, route(1, 0))
-    early = spread(jnp.stack([factor_bank[0], beside[0]]))
+    pair = jnp.stack([factor_bank[0], moved(factor_bank[0], route(1, 0))])
+    early = spread(pair)
+    beside = moved(after(factor_bank[1:], pair), route(1, 0))
     places = jnp.pad(owner_table[:, 0].astype(jnp.float32), ((0, 4), (0, F - 16)))
-    firsts = [bank[r, 0] for bank in (factor_bank, beside) for r in (1, 3)]
-    following = shifted(jnp.concatenate(firsts + [places], 0), -1)
+    firsts = [bank[r, 0] for bank in (factor_bank[1:], beside) for r in (0, 2)]
+    following = shifted(after(jnp.concatenate(firsts + [places], 0), early[3]), -1)
     next_owner = following[128:132, :16].astype(jnp.int32)
     following = following[:128].reshape(2, 2, 32, F)
-    banks = tuple(zip((factor_bank, beside), following))
-    mid = [jnp.concatenate([bank[1], new[:1], bank[2]], 0) for bank, new in banks]
-    mid = spread(after(jnp.stack(mid), early[1]))
-    late = [jnp.concatenate([bank[3], new[1:]], 0) for bank, new in banks]
-    late = spread(after(jnp.stack(late), mid))
+    banks = tuple(zip((factor_bank[1:], beside), following))
+    mid = [jnp.concatenate([bank[0], new[:1], bank[1]], 0) for bank, new in banks]
+    late = [jnp.concatenate([bank[2], new[1:]], 0) for bank, new in banks]
 
     hi0, lo0 = prep(both_cores(early), placement, owner_table[0], "place0")
     strips, halos = [], []
@@ -283,6 +282,8 @@
         order = after(order, halos[c - 2]) if c > 1 else order
         strips.append(round0(strip, first, width, order, lo0))
         halos.append(exchanged(strips[-1]))
+    mid = spread(jnp.stack(mid))
+    late = spread(after(jnp.stack(late), mid))
     mid = both_cores(list(after(mid, strips[1], halos[0])))
     owners = jnp.concatenate([owner_table[1], next_owner[1:2], owner_table[2]], 0)
     hi12, lo12 = prep(mid, placement, owners, "place12")

time: 158 us -> 150 us (0.949)
  waiting for transfers between devices: 68.9 us -> 55.5 us
  starting transfers between devices: 46.2 us -> 50.9 us
    ppermute x13, waiting for transfers between devices: 34.4 us -> 9.91 us  [shifted(): lax.ppermute(value, 'sec', [(i, (i + steps) % count) for i in range(count)])]
    ppermute x22 -> x23, waiting for transfers between devices: 34.5 us -> 45.6 us  [moved(): return lax.ppermute(value, 'col', [(i, target(i)) for i in range(16)])]
    ppermute x13, starting transfers between devices: 25.2 us -> 28.1 us  [shifted(): lax.ppermute(value, 'sec', [(i, (i + steps) % count) for i in range(count)])]
    ppermute x22 -> x23, starting transfers between devices: 20.9 us -> 22.8 us  [moved(): return lax.ppermute(value, 'col', [(i, target(i)) for i in range(16)])]
  transfers between devices with their start and end apart: 35 -> 36, of which waited for: 13 -> 13; matrix products, arithmetic and copies ran while one was open for 2% -> 2% of each run, Pallas kernels for 23% -> 24%
where the time goes in v1:
time: 150 us; the launch traced here: 149 us
  waiting for transfers between devices  55.5 us (37%)
  starting transfers between devices  50.9 us (34%)
  Pallas kernels  38.3 us (26%)
  local copies, waits for them, and re-layouts  3.95 us (3%)
    ppermute x23, waiting for transfers between devices, moved(): return lax.ppermute(value, 'col', [(i, target(i)) for i in range(16)])  45.6 us
    pallas_call x12, Pallas kernels, kernel(): pl.pallas_call(body, in_specs=in_specs, out_specs=out_specs, out_shape=ou...  38.3 us
    ppermute x13, starting transfers between devices, shifted(): lax.ppermute(value, 'sec', [(i, (i + steps) % count) for i in range(count)])  28.1 us
    ppermute x23, starting transfers between devices, moved(): return lax.ppermute(value, 'col', [(i, target(i)) for i in range(16)])  22.8 us
    ppermute x13, waiting for transfers between devices, shifted(): lax.ppermute(value, 'sec', [(i, (i + steps) % count) for i in range(count)])  9.91 us
  transfers between devices with their start and end apart: 36, of which 13 were waited for; matrix products, arithmetic and copies ran while one was open for 2% of the time, Pallas kernels for 24%

profile of v1, /device:TPU:0, one launch (start us, length us, event | category | flops | bytes accessed | tf_op | source)
XLA Modules:
  0.0 149.4 jit_solution(18145323388064107804)
XLA Ops:
  0.0 1.2 slice_bitcast_fusion.3
  1.2 3.2 %collective-permute-start = (f32[2,32,512]{2,1,0:T(8,128)S(1)}, f32[2,32,512]{2,1,0:T(8,128)S(1)}, u32[]{:S(2)}, u32[]{:S(2)}) collective-permute-start(f32[2,32,512]{2,1,0:T(8,128)S(1)} %get-tuple-element.90), channel_id=1, source_target_pairs={{0,8},{1,9},{2,10},{3,11},{4,12},{5,13},{6,14},{7,15},{8,0},{9,1},... | collective-permute-start | bytes 393224 | tf_op jit(solution)/shard_map/ppermute | solution.py:22
  4.4 1.0 slice.106
  5.4 0.8 bitcast_dynamic-update-slice_fusion.1
  6.2 1.6 %collective-permute-done = f32[2,32,512]{2,1,0:T(8,128)S(1)} collective-permute-done((f32[2,32,512]{2,1,0:T(8,128)S(1)}, f32[2,32,512]{2,1,0:T(8,128)S(1)}, u32[]{:S(2)}, u32[]{:S(2)}) %collective-permute-start) | collective-permute-done | bytes 131104 | tf_op jit(solution)/shard_map/ppermute | solution.py:22
  7.9 4.2 %collective-permute-start.3 = (f32[2,2,32,512]{3,2,1,0:T(8,128)S(1)}, f32[2,2,32,512]{3,2,1,0:T(8,128)S(1)}, u32[]{:S(2)}, u32[]{:S(2)}) collective-permute-start(f32[2,2,32,512]{3,2,1,0:T(8,128)S(1)} %pad_maximum_fusion.2.refs_0_), channel_id=1, source_target_pairs={{0,4},{1,5},{2,6},{3,7},{4,0},{5,1},{6,2},{7,3},{8,12},{9,13},{10,... | collective-permute-start | bytes 786440 | tf_op jit(solution)/shard_map/ppermute | solution.py:22
  12.1 0.7 collective-permute-start.2
  12.8 1.3 collective-permute-start.1
  14.1 3.0 %collective-permute-start.12 = (f32[3,2,32,512]{3,2,1,0:T(8,128)S(1)}, f32[3,2,32,512]{3,2,1,0:T(8,128)S(1)}, u32[]{:S(2)}, u32[]{:S(2)}) collective-permute-start(f32[3,2,32,512]{3,2,1,0:T(8,128)S(1)} %slice.106), channel_id=1, source_target_pairs={{0,8},{1,9},{2,10},{3,11},{4,12},{5,13},{6,14},{7,15},{8,0},{9,1},... | collective-permute-start | bytes 1179656 | tf_op jit(solution)/shard_map/ppermute | solution.py:22
  17.1 0.8 bitcast_dynamic-update-slice_fusion
  18.0 1.3 collective-permute-done.3.refs_3_
  19.3 4.6 %collective-permute-done.2.refs_2_ = f32[2,2,32,512]{3,2,1,0:T(8,128)S(1)} collective-permute-done((f32[2,2,32,512]{3,2,1,0:T(8,128)S(1)}, f32[2,2,32,512]{3,2,1,0:T(8,128)S(1)}, u32[]{:S(2)}, u32[]{:S(2)}) %collective-permute-start.2) | collective-permute-done | bytes 262176 | tf_op jit(solution)/shard_map/ppermute | solution.py:22
  23.9 0.5 collective-permute-start.5
  24.8 4.0 %collective-permute-start.13 = (f32[136,512]{1,0:T(8,128)S(1)}, f32[136,512]{1,0:T(8,128)S(1)}, u32[]{:S(2)}, u32[]{:S(2)}) collective-permute-start(f32[136,512]{1,0:T(8,128)S(1)} %pad_dynamic-update-slice_fusion), channel_id=1, source_target_pairs={{0,112},{16,0},{32,16},{48,32},{64,48},{80,64},{96,80},{112,96},{1... | collective-permute-start | bytes 835592 | tf_op jit(solution)/shard_map/ppermute | solution.py:18
  28.8 0.9 place0.1
  29.7 5.2 %round0.3 = (f32[256,1024]{1,0:T(8,128)S(1)}, f32[512,1024]{1,0:T(8,128)S(1)}, f32[256,1024]{1,0:T(8,128)S(1)}) custom-call(f32[1024,2048]{1,0:T(8,128)} %x_ref.5, bf16[2,512,512]{2,1,0:T(8,128)(2,1)S(1)} %get-tuple-element.54.hi_ref, bf16[2,512,512]{2,1,0:T(8,128)(2,1)S(1)} %get-tuple-element.48.lo_ref), custom_call_target="tpu_custom_call" | custom-call | flops 32212254 | bytes 20971 | tf_op jit(solution)/shard_map/round0/pallas_call | solution.py:38
  35.0 4.1 %collective-permute-start.9 = (f32[256,1024]{1,0:T(8,128)S(1)}, f32[256,1024]{1,0:T(8,128)S(1)}, u32[]{:S(2)}, u32[]{:S(2)}) collective-permute-start(f32[256,1024]{1,0:T(8,128)S(1)} %get-tuple-element.49.h0_ref), channel_id=1, source_target_pairs={{0,112},{16,0},{32,16},{48,32},{64,48},{80,64},{96,80},{112,96},{1... | collective-permute-start | bytes 3145736 | tf_op jit(solution)/shard_map/ppermute | solution.py:18
  39.3 1.7 %collective-permute-start.16 = (f32[2,5,32,512]{3,2,1,0:T(8,128)S(1)}, f32[2,5,32,512]{3,2,1,0:T(8,128)S(1)}, u32[]{:S(2)}, u32[]{:S(2)}) collective-permute-start(f32[2,5,32,512]{3,2,1,0:T(8,128)S(1)} %pad_maximum_fusion.refs_0_), channel_id=1, source_target_pairs={{0,4},{1,5},{2,6},{3,7},{4,0},{5,1},{6,2},{7,3},{8,12},{9,13},{10,... | collective-permute-start | bytes 1966088 | tf_op jit(solution)/shard_map/ppermute | solution.py:22
  41.0 2.0 %collective-permute-start.15 = (f32[2,5,32,512]{3,2,1,0:T(8,128)S(1)}, f32[2,5,32,512]{3,2,1,0:T(8,128)S(1)}, u32[]{:S(2)}, u32[]{:S(2)}) collective-permute-start(f32[2,5,32,512]{3,2,1,0:T(8,128)S(1)} %pad_maximum_fusion.refs_0_), channel_id=1, source_target_pairs={{0,6},{1,7},{2,0},{3,1},{4,2},{5,3},{6,4},{7,5},{8,14},{9,15},{10,... | collective-permute-start | bytes 1966088 | tf_op jit(solution)/shard_map/ppermute | solution.py:22
  43.0 3.2 %round0.4 = (f32[256,512]{1,0:T(8,128)S(1)}, f32[512,512]{1,0:T(8,128)S(1)}, f32[256,512]{1,0:T(8,128)S(1)}) custom-call(f32[1024,2048]{1,0:T(8,128)} %x_ref.5, bf16[2,512,512]{2,1,0:T(8,128)(2,1)S(1)} %get-tuple-element.54.hi_ref, bf16[2,512,512]{2,1,0:T(8,128)(2,1)S(1)} %get-tuple-element.48.lo_ref), custom_call_target="tpu_custom_call" | custom-call | flops 16106127 | bytes 20971 | tf_op jit(solution)/shard_map/round0/pallas_call | solution.py:38
  46.3 12.3 %collective-permute-done.16.refs_3_ = f32[2,5,32,512]{3,2,1,0:T(8,128)S(1)} collective-permute-done((f32[2,5,32,512]{3,2,1,0:T(8,128)S(1)}, f32[2,5,32,512]{3,2,1,0:T(8,128)S(1)}, u32[]{:S(2)}, u32[]{:S(2)}) %collective-permute-start.16) | collective-permute-done | bytes 655392 | tf_op jit(solution)/shard_map/ppermute | solution.py:22
  58.6 11.8 %collective-permute-done.15.refs_2_ = f32[2,5,32,512]{3,2,1,0:T(8,128)S(1)} collective-permute-done((f32[2,5,32,512]{3,2,1,0:T(8,128)S(1)}, f32[2,5,32,512]{3,2,1,0:T(8,128)S(1)}, u32[]{:S(2)}, u32[]{:S(2)}) %collective-permute-start.15) | collective-permute-done | bytes 655392 | tf_op jit(solution)/shard_map/ppermute | solution.py:22
  70.5 0.5 collective-permute-start.18
  71.5 1.1 collective-permute-done.17.refs_4_
  72.6 3.1 %collective-permute-start.22 = (f32[256,512]{1,0:T(8,128)S(1)}, f32[256,512]{1,0:T(8,128)S(1)}, u32[]{:S(2)}, u32[]{:S(2)}) collective-permute-start(f32[256,512]{1,0:T(8,128)S(1)} %get-tuple-element.51.h0_ref), channel_id=1, source_target_pairs={{0,112},{16,0},{32,16},{48,32},{64,48},{80,64},{96,80},{112,96},{1... | collective-permute-start | bytes 1572872 | tf_op jit(solution)/shard_map/ppermute | solution.py:18
  75.6 3.2 %round0.5 = (f32[256,512]{1,0:T(8,128)S(1)}, f32[512,512]{1,0:T(8,128)S(1)}, f32[256,512]{1,0:T(8,128)S(1)}) custom-call(f32[1024,2048]{1,0:T(8,128)} %x_ref.5, bf16[2,512,512]{2,1,0:T(8,128)(2,1)S(1)} %get-tuple-element.54.hi_ref, bf16[2,512,512]{2,1,0:T(8,128)(2,1)S(1)} %get-tuple-element.48.lo_ref), custom_call_target="tpu_custom_call" | custom-call | flops 16106127 | bytes 20971 | tf_op jit(solution)/shard_map/round0/pallas_call | solution.py:38
  78.9 4.1 %collective-permute-start.11 = (f32[256,512]{1,0:T(8,128)S(1)}, f32[256,512]{1,0:T(8,128)S(1)}, u32[]{:S(2)}, u32[]{:S(2)}) collective-permute-start(f32[256,512]{1,0:T(8,128)S(1)} %get-tuple-element.56.h0_ref), channel_id=1, source_target_pairs={{0,112},{16,0},{32,16},{48,32},{64,48},{80,64},{96,80},{112,96},{1... | collective-permute-start | bytes 1572872 | tf_op jit(solution)/shard_map/ppermute | solution.py:18
  83.1 1.3 place12.1
  84.4 4.0 %collective-permute-done.21.a_ref = f32[256,512]{1,0:T(8,128)S(1)} collective-permute-done((f32[256,512]{1,0:T(8,128)S(1)}, f32[256,512]{1,0:T(8,128)S(1)}, u32[]{:S(2)}, u32[]{:S(2)}) %collective-permute-start.21) | collective-permute-done | bytes 524320 | tf_op jit(solution)/shard_map/ppermute | solution.py:18
  88.4 6.7 %rounds12.3 = (f32[256,1024]{1,0:T(8,128)S(1)}, f32[512,1024]{1,0:T(8,128)S(1)}, f32[256,1024]{1,0:T(8,128)S(1)}) custom-call(f32[256,1024]{1,0:T(8,128)S(1)} %collective-permute-done.8.a_ref, f32[256,1024]{1,0:T(8,128)S(1)} %get-tuple-element.49.h0_ref, f32[512,1024]{1,0:T(8,128)S(1)} %get-tuple-element.67.h12_ref, ...), custom_call_target="tpu_custom_call" | custom-call | flops 64424508 | bytes 115343 | tf_op jit(solution)/shard_map/rounds12/pallas_call | solution.py:38
  95.2 4.2 %collective-permute-start.24 = (f32[256,1024]{1,0:T(8,128)S(1)}, f32[256,1024]{1,0:T(8,128)S(1)}, u32[]{:S(2)}, u32[]{:S(2)}) collective-permute-start(f32[256,1024]{1,0:T(8,128)S(1)} %get-tuple-element.70.h0_ref), channel_id=1, source_target_pairs={{0,112},{16,0},{32,16},{48,32},{64,48},{80,64},{96,80},{112,96},{1... | collective-permute-start | bytes 3145736 | tf_op jit(solution)/shard_map/ppermute | solution.py:18
  99.5 2.5 %collective-permute-start.29 = (f32[2,3,32,512]{3,2,1,0:T(8,128)S(1)}, f32[2,3,32,512]{3,2,1,0:T(8,128)S(1)}, u32[]{:S(2)}, u32[]{:S(2)}) collective-permute-start(f32[2,3,32,512]{3,2,1,0:T(8,128)S(1)} %pad_maximum_fusion.1.refs_0_), channel_id=1, source_target_pairs={{0,4},{1,5},{2,6},{3,7},{4,0},{5,1},{6,2},{7,3},{8,12},{9,13},{10,... | collective-permute-start | bytes 1179656 | tf_op jit(solution)/shard_map/ppermute | solution.py:22
  102.0 1.3 collective-permute-start.28
  103.2 0.7 collective-permute-start.27
  104.0 3.4 %rounds12.4 = (f32[256,512]{1,0:T(8,128)S(1)}, f32[512,512]{1,0:T(8,128)S(1)}, f32[256,512]{1,0:T(8,128)S(1)}) custom-call(f32[256,512]{1,0:T(8,128)S(1)} %collective-permute-done.21.a_ref, f32[256,512]{1,0:T(8,128)S(1)} %get-tuple-element.51.h0_ref, f32[512,512]{1,0:T(8,128)S(1)} %get-tuple-element.60.h12_ref, f32[256,512]{1,0:T(8,128)S(1)} %get-tuple-element.61.h3_ref, ...), custom_call_target="tpu_custom_call" | custom-call | flops 32212254 | bytes 83886 | tf_op jit(solution)/shard_map/rounds12/pallas_call | solution.py:38
  107.4 5.7 %collective-permute-done.29.refs_3_ = f32[2,3,32,512]{3,2,1,0:T(8,128)S(1)} collective-permute-done((f32[2,3,32,512]{3,2,1,0:T(8,128)S(1)}, f32[2,3,32,512]{3,2,1,0:T(8,128)S(1)}, u32[]{:S(2)}, u32[]{:S(2)}) %collective-permute-start.29) | collective-permute-done | bytes 393248 | tf_op jit(solution)/shard_map/ppermute | solution.py:22
  113.2 5.1 %collective-permute-done.28.refs_2_ = f32[2,3,32,512]{3,2,1,0:T(8,128)S(1)} collective-permute-done((f32[2,3,32,512]{3,2,1,0:T(8,128)S(1)}, f32[2,3,32,512]{3,2,1,0:T(8,128)S(1)}, u32[]{:S(2)}, u32[]{:S(2)}) %collective-permute-start.28) | collective-permute-done | bytes 393248 | tf_op jit(solution)/shard_map/ppermute | solution.py:22
  118.2 0.5 collective-permute-start.31
  118.7 2.5 %collective-permute-done.23.a_ref = f32[256,1024]{1,0:T(8,128)S(1)} collective-permute-done((f32[256,1024]{1,0:T(8,128)S(1)}, f32[256,1024]{1,0:T(8,128)S(1)}, u32[]{:S(2)}, u32[]{:S(2)}) %collective-permute-start.23) | collective-permute-done | bytes 1048608 | tf_op jit(solution)/shard_map/ppermute | solution.py:18
  121.2 4.1 %collective-permute-start.35 = (f32[256,512]{1,0:T(8,128)S(1)}, f32[256,512]{1,0:T(8,128)S(1)}, u32[]{:S(2)}, u32[]{:S(2)}) collective-permute-start(f32[256,512]{1,0:T(8,128)S(1)} %get-tuple-element.72.h0_ref), channel_id=1, source_target_pairs={{0,112},{16,0},{32,16},{48,32},{64,48},{80,64},{96,80},{112,96},{1... | collective-permute-start | bytes 1572872 | tf_op jit(solution)/shard_map/ppermute | solution.py:18
  125.4 3.4 %rounds12.5 = (f32[256,512]{1,0:T(8,128)S(1)}, f32[512,512]{1,0:T(8,128)S(1)}, f32[256,512]{1,0:T(8,128)S(1)}) custom-call(f32[256,512]{1,0:T(8,128)S(1)} %collective-permute-done.10.a_ref, f32[256,512]{1,0:T(8,128)S(1)} %get-tuple-element.56.h0_ref, f32[512,512]{1,0:T(8,128)S(1)} %get-tuple-element.57.h12_ref, f32[256,512]{1,0:T(8,128)S(1)} %get-tuple-element.55.h3_ref, ...), custom_call_target="tpu_custom_call" | custom-call | flops 32212254 | bytes 83886 | tf_op jit(solution)/shard_map/rounds12/pallas_call | solution.py:38
  128.9 4.1 %collective-permute-start.26 = (f32[256,512]{1,0:T(8,128)S(1)}, f32[256,512]{1,0:T(8,128)S(1)}, u32[]{:S(2)}, u32[]{:S(2)}) collective-permute-start(f32[256,512]{1,0:T(8,128)S(1)} %get-tuple-element.77.h0_ref), channel_id=1, source_target_pairs={{0,112},{16,0},{32,16},{48,32},{64,48},{80,64},{96,80},{112,96},{1... | collective-permute-start | bytes 1572872 | tf_op jit(solution)/shard_map/ppermute | solution.py:18
  133.0 1.7 %collective-permute-done.33.refs_7_ = f32[2,3,32,512]{3,2,1,0:T(8,128)S(1)} collective-permute-done((f32[2,3,32,512]{3,2,1,0:T(8,128)S(1)}, f32[2,3,32,512]{3,2,1,0:T(8,128)S(1)}, u32[]{:S(2)}, u32[]{:S(2)}) %collective-permute-start.33) | collective-permute-done | bytes 393248 | tf_op jit(solution)/shard_map/ppermute | solution.py:22
  134.7 1.0 place3.1
  135.8 4.5 %round3.3.rest_0_ = f32[1024,2048]{1,0:T(8,128)} custom-call(f32[256,1024]{1,0:T(8,128)S(1)} %collective-permute-done.23.a_ref, f32[256,1024]{1,0:T(8,128)S(1)} %get-tuple-element.70.h0_ref, f32[512,1024]{1,0:T(8,128)S(1)} %get-tuple-element.88.h12_ref, f32[256,1024]{1,0:T(8,128)S(1)} %get-tuple-element.74.h3_ref, ...), custom_call_target="tpu_custom_call" | custom-call | flops 32212254 | bytes 94371 | tf_op jit(solution)/shard_map/round3/pallas_call | solution.py:38
  140.3 2.7 %round3.4.rest_0_ = f32[1024,2048]{1,0:T(8,128)} custom-call(f32[256,512]{1,0:T(8,128)S(1)} %collective-permute-done.34.a_ref, f32[256,512]{1,0:T(8,128)S(1)} %get-tuple-element.72.h0_ref, f32[512,512]{1,0:T(8,128)S(1)} %get-tuple-element.80.h12_ref, f32[256,512]{1,0:T(8,128)S(1)} %get-tuple-element.81.h3_ref, ...), custom_call_target="tpu_custom_call", output_to_operand_aliasing={{}: (7, {})} | custom-call | flops 16106127 | bytes 62914 | tf_op jit(solution)/shard_map/round3/pallas_call | solution.py:38
  143.0 3.4 %collective-permute-done.25.a_ref = f32[256,512]{1,0:T(8,128)S(1)} collective-permute-done((f32[256,512]{1,0:T(8,128)S(1)}, f32[256,512]{1,0:T(8,128)S(1)}, u32[]{:S(2)}, u32[]{:S(2)}) %collective-permute-start.25) | collective-permute-done | bytes 524320 | tf_op jit(solution)/shard_map/ppermute | solution.py:18
  146.4 2.7 %round3.5 = f32[1024,2048]{1,0:T(8,128)} custom-call(f32[256,512]{1,0:T(8,128)S(1)} %collective-permute-done.25.a_ref, f32[256,512]{1,0:T(8,128)S(1)} %get-tuple-element.77.h0_ref, f32[512,512]{1,0:T(8,128)S(1)} %get-tuple-element.78.h12_ref, f32[256,512]{1,0:T(8,128)S(1)} %get-tuple-element.76.h3_ref, ...), custom_call_target="tpu_custom_call", output_to_operand_aliasing={{}: (7, {})} | custom-call | flops 16106127 | bytes 62914 | tf_op jit(solution)/shard_map/round3/pallas_call | solution.py:38
  (60 shorter events, 1.6 us)
Async XLA Ops:
  0.0 17.1 %copy-start = (s32[4,2,16]{2,1,0:T(2,128)S(1)}, s32[4,2,16]{2,1,0:T(2,128)}, u32[]{:S(2)}) copy-start(s32[4,2,16]{2,1,0:T(2,128)} %param.5) | copy-start | bytes 1540
  1.2 6.7 %collective-permute-start = (f32[2,32,512]{2,1,0:T(8,128)S(1)}, f32[2,32,512]{2,1,0:T(8,128)S(1)}, u32[]{:S(2)}, u32[]{:S(2)}) collective-permute-start(f32[2,32,512]{2,1,0:T(8,128)S(1)} %get-tuple-element.90), channel_id=1, source_target_pairs={{0,8},{1,9},{2,10},{3,11},{4,12},{5,13},{6,14},{7,15},{8,0},{9,1},... | collective-permute-start | bytes 393224 | tf_op jit(solution)/shard_map/ppermute | solution.py:22
  7.9 11.4 %collective-permute-start.3 = (f32[2,2,32,512]{3,2,1,0:T(8,128)S(1)}, f32[2,2,32,512]{3,2,1,0:T(8,128)S(1)}, u32[]{:S(2)}, u32[]{:S(2)}) collective-permute-start(f32[2,2,32,512]{3,2,1,0:T(8,128)S(1)} %pad_maximum_fusion.2.refs_0_), channel_id=1, source_target_pairs={{0,4},{1,5},{2,6},{3,7},{4,0},{5,1},{6,2},{7,3},{8,12},{9,13},{10,... | collective-permute-start | bytes 786440 | tf_op jit(solution)/shard_map/ppermute | solution.py:22
  12.1 11.8 %collective-permute-start.2 = (f32[2,2,32,512]{3,2,1,0:T(8,128)S(1)}, f32[2,2,32,512]{3,2,1,0:T(8,128)S(1)}, u32[]{:S(2)}, u32[]{:S(2)}) collective-permute-start(f32[2,2,32,512]{3,2,1,0:T(8,128)S(1)} %pad_maximum_fusion.2.refs_0_), channel_id=1, source_target_pairs={{0,6},{1,7},{2,0},{3,1},{4,2},{5,3},{6,4},{7,5},{8,14},{9,15},{10,... | collective-permute-start | bytes 786440 | tf_op jit(solution)/shard_map/ppermute | solution.py:22
  12.8 11.1 %collective-permute-start.1 = (f32[2,2,32,512]{3,2,1,0:T(8,128)S(1)}, f32[2,2,32,512]{3,2,1,0:T(8,128)S(1)}, u32[]{:S(2)}, u32[]{:S(2)}) collective-permute-start(f32[2,2,32,512]{3,2,1,0:T(8,128)S(1)} %pad_maximum_fusion.2.refs_0_), channel_id=1, source_target_pairs={{0,2},{1,3},{2,4},{3,5},{4,6},{5,7},{6,0},{7,1},{8,10},{9,11},{10,... | collective-permute-start | bytes 786440 | tf_op jit(solution)/shard_map/ppermute | solution.py:22
  14.1 10.6 %collective-permute-start.12 = (f32[3,2,32,512]{3,2,1,0:T(8,128)S(1)}, f32[3,2,32,512]{3,2,1,0:T(8,128)S(1)}, u32[]{:S(2)}, u32[]{:S(2)}) collective-permute-start(f32[3,2,32,512]{3,2,1,0:T(8,128)S(1)} %slice.106), channel_id=1, source_target_pairs={{0,8},{1,9},{2,10},{3,11},{4,12},{5,13},{6,14},{7,15},{8,0},{9,1},... | collective-permute-start | bytes 1179656 | tf_op jit(solution)/shard_map/ppermute | solution.py:22
  18.0 10.9 %collective-permute-start.4 = (f32[2,2,32,512]{3,2,1,0:T(8,128)S(1)}, f32[2,2,32,512]{3,2,1,0:T(8,128)S(1)}, u32[]{:S(2)}, u32[]{:S(2)}) collective-permute-start(f32[2,2,32,512]{3,2,1,0:T(8,128)S(1)} %pad_maximum_fusion.2.refs_0_), channel_id=1, source_target_pairs={{0,1},{1,0},{2,3},{3,2},{4,5},{5,4},{6,7},{7,6},{8,9},{9,8},{10,11... | collective-permute-start | bytes 786440 | tf_op jit(solution)/shard_map/ppermute | solution.py:22
  19.3 9.5 %collective-permute-start.7 = (f32[2,2,32,512]{3,2,1,0:T(8,128)S(1)}, f32[2,2,32,512]{3,2,1,0:T(8,128)S(1)}, u32[]{:S(2)}, u32[]{:S(2)}) collective-permute-start(f32[2,2,32,512]{3,2,1,0:T(8,128)S(1)} %collective-permute-done.3.refs_3_), channel_id=1, source_target_pairs={{0,1},{1,0},{2,3},{3,2},{4,5},{5,4},{6,7},{7,6},{8,9},{9,8},{10,11... | collective-permute-start | bytes 786440 | tf_op jit(solution)/shard_map/ppermute | solution.py:22
  23.9 4.9 %collective-permute-start.6 = (f32[2,2,32,512]{3,2,1,0:T(8,128)S(1)}, f32[2,2,32,512]{3,2,1,0:T(8,128)S(1)}, u32[]{:S(2)}, u32[]{:S(2)}) collective-permute-start(f32[2,2,32,512]{3,2,1,0:T(8,128)S(1)} %collective-permute-done.2.refs_2_), channel_id=1, source_target_pairs={{0,1},{1,0},{2,3},{3,2},{4,5},{5,4},{6,7},{7,6},{8,9},{9,8},{10,11... | collective-permute-start | bytes 786440 | tf_op jit(solution)/shard_map/ppermute | solution.py:22
  23.9 5.0 %collective-permute-start.5 = (f32[2,2,32,512]{3,2,1,0:T(8,128)S(1)}, f32[2,2,32,512]{3,2,1,0:T(8,128)S(1)}, u32[]{:S(2)}, u32[]{:S(2)}) collective-permute-start(f32[2,2,32,512]{3,2,1,0:T(8,128)S(1)} %collective-permute-done.1.refs_1_), channel_id=1, source_target_pairs={{0,1},{1,0},{2,3},{3,2},{4,5},{5,4},{6,7},{7,6},{8,9},{9,8},{10,11... | collective-permute-start | bytes 786440 | tf_op jit(solution)/shard_map/ppermute | solution.py:22
  24.8 14.4 %collective-permute-start.13 = (f32[136,512]{1,0:T(8,128)S(1)}, f32[136,512]{1,0:T(8,128)S(1)}, u32[]{:S(2)}, u32[]{:S(2)}) collective-permute-start(f32[136,512]{1,0:T(8,128)S(1)} %pad_dynamic-update-slice_fusion), channel_id=1, source_target_pairs={{0,112},{16,0},{32,16},{48,32},{64,48},{80,64},{96,80},{112,96},{1... | collective-permute-start | bytes 835592 | tf_op jit(solution)/shard_map/ppermute | solution.py:18
  34.9 35.5 %collective-permute-start.8 = (f32[256,1024]{1,0:T(8,128)S(1)}, f32[256,1024]{1,0:T(8,128)S(1)}, u32[]{:S(2)}, u32[]{:S(2)}) collective-permute-start(f32[256,1024]{1,0:T(8,128)S(1)} %get-tuple-element.53.h3_ref), channel_id=1, source_target_pairs={{0,16},{16,32},{32,48},{48,64},{64,80},{80,96},{96,112},{112,0},{1... | collective-permute-start | bytes 3145736 | tf_op jit(solution)/shard_map/ppermute | solution.py:18
  35.0 35.4 %collective-permute-start.9 = (f32[256,1024]{1,0:T(8,128)S(1)}, f32[256,1024]{1,0:T(8,128)S(1)}, u32[]{:S(2)}, u32[]{:S(2)}) collective-permute-start(f32[256,1024]{1,0:T(8,128)S(1)} %get-tuple-element.49.h0_ref), channel_id=1, source_target_pairs={{0,112},{16,0},{32,16},{48,32},{64,48},{80,64},{96,80},{112,96},{1... | collective-permute-start | bytes 3145736 | tf_op jit(solution)/shard_map/ppermute | solution.py:18
  39.3 19.3 %collective-permute-start.16 = (f32[2,5,32,512]{3,2,1,0:T(8,128)S(1)}, f32[2,5,32,512]{3,2,1,0:T(8,128)S(1)}, u32[]{:S(2)}, u32[]{:S(2)}) collective-permute-start(f32[2,5,32,512]{3,2,1,0:T(8,128)S(1)} %pad_maximum_fusion.refs_0_), channel_id=1, source_target_pairs={{0,4},{1,5},{2,6},{3,7},{4,0},{5,1},{6,2},{7,3},{8,12},{9,13},{10,... | collective-permute-start | bytes 1966088 | tf_op jit(solution)/shard_map/ppermute | solution.py:22
  41.0 29.4 %collective-permute-start.15 = (f32[2,5,32,512]{3,2,1,0:T(8,128)S(1)}, f32[2,5,32,512]{3,2,1,0:T(8,128)S(1)}, u32[]{:S(2)}, u32[]{:S(2)}) collective-permute-start(f32[2,5,32,512]{3,2,1,0:T(8,128)S(1)} %pad_maximum_fusion.refs_0_), channel_id=1, source_target_pairs={{0,6},{1,7},{2,0},{3,1},{4,2},{5,3},{6,4},{7,5},{8,14},{9,15},{10,... | collective-permute-start | bytes 1966088 | tf_op jit(solution)/shard_map/ppermute | solution.py:22
  43.0 27.3 %collective-permute-start.14 = (f32[2,5,32,512]{3,2,1,0:T(8,128)S(1)}, f32[2,5,32,512]{3,2,1,0:T(8,128)S(1)}, u32[]{:S(2)}, u32[]{:S(2)}) collective-permute-start(f32[2,5,32,512]{3,2,1,0:T(8,128)S(1)} %pad_maximum_fusion.refs_0_), channel_id=1, source_target_pairs={{0,2},{1,3},{2,4},{3,5},{4,6},{5,7},{6,0},{7,1},{8,10},{9,11},{10,... | collective-permute-start | bytes 1966088 | tf_op jit(solution)/shard_map/ppermute | solution.py:22
  70.4 2.2 %collective-permute-start.17 = (f32[2,5,32,512]{3,2,1,0:T(8,128)S(1)}, f32[2,5,32,512]{3,2,1,0:T(8,128)S(1)}, u32[]{:S(2)}, u32[]{:S(2)}) collective-permute-start(f32[2,5,32,512]{3,2,1,0:T(8,128)S(1)} %pad_maximum_fusion.refs_0_), channel_id=1, source_target_pairs={{0,1},{1,0},{2,3},{3,2},{4,5},{5,4},{6,7},{7,6},{8,9},{9,8},{10,11... | collective-permute-start | bytes 1966088 | tf_op jit(solution)/shard_map/ppermute | solution.py:22
  70.5 8.4 %collective-permute-start.18 = (f32[2,5,32,512]{3,2,1,0:T(8,128)S(1)}, f32[2,5,32,512]{3,2,1,0:T(8,128)S(1)}, u32[]{:S(2)}, u32[]{:S(2)}) collective-permute-start(f32[2,5,32,512]{3,2,1,0:T(8,128)S(1)} %collective-permute-done.14.refs_1_), channel_id=1, source_target_pairs={{0,1},{1,0},{2,3},{3,2},{4,5},{5,4},{6,7},{7,6},{8,9},{9,8},{10,11... | collective-permute-start | bytes 1966088 | tf_op jit(solution)/shard_map/ppermute | solution.py:22
  71.0 8.0 %collective-permute-start.19 = (f32[2,5,32,512]{3,2,1,0:T(8,128)S(1)}, f32[2,5,32,512]{3,2,1,0:T(8,128)S(1)}, u32[]{:S(2)}, u32[]{:S(2)}) collective-permute-start(f32[2,5,32,512]{3,2,1,0:T(8,128)S(1)} %collective-permute-done.15.refs_2_), channel_id=1, source_target_pairs={{0,1},{1,0},{2,3},{3,2},{4,5},{5,4},{6,7},{7,6},{8,9},{9,8},{10,11... | collective-permute-start | bytes 1966088 | tf_op jit(solution)/shard_map/ppermute | solution.py:22
  71.1 12.0 %collective-permute-start.20 = (f32[2,5,32,512]{3,2,1,0:T(8,128)S(1)}, f32[2,5,32,512]{3,2,1,0:T(8,128)S(1)}, u32[]{:S(2)}, u32[]{:S(2)}) collective-permute-start(f32[2,5,32,512]{3,2,1,0:T(8,128)S(1)} %collective-permute-done.16.refs_3_), channel_id=1, source_target_pairs={{0,1},{1,0},{2,3},{3,2},{4,5},{5,4},{6,7},{7,6},{8,9},{9,8},{10,11... | collective-permute-start | bytes 1966088 | tf_op jit(solution)/shard_map/ppermute | solution.py:22
  71.5 16.9 %collective-permute-start.21 = (f32[256,512]{1,0:T(8,128)S(1)}, f32[256,512]{1,0:T(8,128)S(1)}, u32[]{:S(2)}, u32[]{:S(2)}) collective-permute-start(f32[256,512]{1,0:T(8,128)S(1)} %get-tuple-element.61.h3_ref), channel_id=1, source_target_pairs={{0,16},{16,32},{32,48},{48,64},{64,80},{80,96},{96,112},{112,0},{1... | collective-permute-start | bytes 1572872 | tf_op jit(solution)/shard_map/ppermute | solution.py:18
  72.6 15.8 %collective-permute-start.22 = (f32[256,512]{1,0:T(8,128)S(1)}, f32[256,512]{1,0:T(8,128)S(1)}, u32[]{:S(2)}, u32[]{:S(2)}) collective-permute-start(f32[256,512]{1,0:T(8,128)S(1)} %get-tuple-element.51.h0_ref), channel_id=1, source_target_pairs={{0,112},{16,0},{32,16},{48,32},{64,48},{80,64},{96,80},{112,96},{1... | collective-permute-start | bytes 1572872 | tf_op jit(solution)/shard_map/ppermute | solution.py:18
  78.9 23.1 %collective-permute-start.10 = (f32[256,512]{1,0:T(8,128)S(1)}, f32[256,512]{1,0:T(8,128)S(1)}, u32[]{:S(2)}, u32[]{:S(2)}) collective-permute-start(f32[256,512]{1,0:T(8,128)S(1)} %get-tuple-element.55.h3_ref), channel_id=1, source_target_pairs={{0,16},{16,32},{32,48},{48,64},{64,80},{80,96},{96,112},{112,0},{1... | collective-permute-start | bytes 1572872 | tf_op jit(solution)/shard_map/ppermute | solution.py:18
  78.9 24.3 %collective-permute-start.11 = (f32[256,512]{1,0:T(8,128)S(1)}, f32[256,512]{1,0:T(8,128)S(1)}, u32[]{:S(2)}, u32[]{:S(2)}) collective-permute-start(f32[256,512]{1,0:T(8,128)S(1)} %get-tuple-element.56.h0_ref), channel_id=1, source_target_pairs={{0,112},{16,0},{32,16},{48,32},{64,48},{80,64},{96,80},{112,96},{1... | collective-permute-start | bytes 1572872 | tf_op jit(solution)/shard_map/ppermute | solution.py:18
  95.1 26.2 %collective-permute-start.23 = (f32[256,1024]{1,0:T(8,128)S(1)}, f32[256,1024]{1,0:T(8,128)S(1)}, u32[]{:S(2)}, u32[]{:S(2)}) collective-permute-start(f32[256,1024]{1,0:T(8,128)S(1)} %get-tuple-element.74.h3_ref), channel_id=1, source_target_pairs={{0,16},{16,32},{32,48},{48,64},{64,80},{80,96},{96,112},{112,0},{1... | collective-permute-start | bytes 3145736 | tf_op jit(solution)/shard_map/ppermute | solution.py:18
  95.2 26.1 %collective-permute-start.24 = (f32[256,1024]{1,0:T(8,128)S(1)}, f32[256,1024]{1,0:T(8,128)S(1)}, u32[]{:S(2)}, u32[]{:S(2)}) collective-permute-start(f32[256,1024]{1,0:T(8,128)S(1)} %get-tuple-element.70.h0_ref), channel_id=1, source_target_pairs={{0,112},{16,0},{32,16},{48,32},{64,48},{80,64},{96,80},{112,96},{1... | collective-permute-start | bytes 3145736 | tf_op jit(solution)/shard_map/ppermute | solution.py:18
  99.5 13.7 %collective-permute-start.29 = (f32[2,3,32,512]{3,2,1,0:T(8,128)S(1)}, f32[2,3,32,512]{3,2,1,0:T(8,128)S(1)}, u32[]{:S(2)}, u32[]{:S(2)}) collective-permute-start(f32[2,3,32,512]{3,2,1,0:T(8,128)S(1)} %pad_maximum_fusion.1.refs_0_), channel_id=1, source_target_pairs={{0,4},{1,5},{2,6},{3,7},{4,0},{5,1},{6,2},{7,3},{8,12},{9,13},{10,... | collective-permute-start | bytes 1179656 | tf_op jit(solution)/shard_map/ppermute | solution.py:22
  102.0 16.3 %collective-permute-start.28 = (f32[2,3,32,512]{3,2,1,0:T(8,128)S(1)}, f32[2,3,32,512]{3,2,1,0:T(8,128)S(1)}, u32[]{:S(2)}, u32[]{:S(2)}) collective-permute-start(f32[2,3,32,512]{3,2,1,0:T(8,128)S(1)} %pad_maximum_fusion.1.refs_0_), channel_id=1, source_target_pairs={{0,6},{1,7},{2,0},{3,1},{4,2},{5,3},{6,4},{7,5},{8,14},{9,15},{10,... | collective-permute-start | bytes 1179656 | tf_op jit(solution)/shard_map/ppermute | solution.py:22
  103.2 15.0 %collective-permute-start.27 = (f32[2,3,32,512]{3,2,1,0:T(8,128)S(1)}, f32[2,3,32,512]{3,2,1,0:T(8,128)S(1)}, u32[]{:S(2)}, u32[]{:S(2)}) collective-permute-start(f32[2,3,32,512]{3,2,1,0:T(8,128)S(1)} %pad_maximum_fusion.1.refs_0_), channel_id=1, source_target_pairs={{0,2},{1,3},{2,4},{3,5},{4,6},{5,7},{6,0},{7,1},{8,10},{9,11},{10,... | collective-permute-start | bytes 1179656 | tf_op jit(solution)/shard_map/ppermute | solution.py:22
  118.2 10.6 %collective-permute-start.30 = (f32[2,3,32,512]{3,2,1,0:T(8,128)S(1)}, f32[2,3,32,512]{3,2,1,0:T(8,128)S(1)}, u32[]{:S(2)}, u32[]{:S(2)}) collective-permute-start(f32[2,3,32,512]{3,2,1,0:T(8,128)S(1)} %pad_maximum_fusion.1.refs_0_), channel_id=1, source_target_pairs={{0,1},{1,0},{2,3},{3,2},{4,5},{5,4},{6,7},{7,6},{8,9},{9,8},{10,11... | collective-permute-start | bytes 1179656 | tf_op jit(solution)/shard_map/ppermute | solution.py:22
  118.2 10.7 %collective-permute-start.31 = (f32[2,3,32,512]{3,2,1,0:T(8,128)S(1)}, f32[2,3,32,512]{3,2,1,0:T(8,128)S(1)}, u32[]{:S(2)}, u32[]{:S(2)}) collective-permute-start(f32[2,3,32,512]{3,2,1,0:T(8,128)S(1)} %collective-permute-done.27.refs_1_), channel_id=1, source_target_pairs={{0,1},{1,0},{2,3},{3,2},{4,5},{5,4},{6,7},{7,6},{8,9},{9,8},{10,11... | collective-permute-start | bytes 1179656 | tf_op jit(solution)/shard_map/ppermute | solution.py:22
  118.7 14.3 %collective-permute-start.32 = (f32[2,3,32,512]{3,2,1,0:T(8,128)S(1)}, f32[2,3,32,512]{3,2,1,0:T(8,128)S(1)}, u32[]{:S(2)}, u32[]{:S(2)}) collective-permute-start(f32[2,3,32,512]{3,2,1,0:T(8,128)S(1)} %collective-permute-done.28.refs_2_), channel_id=1, source_target_pairs={{0,1},{1,0},{2,3},{3,2},{4,5},{5,4},{6,7},{7,6},{8,9},{9,8},{10,11... | collective-permute-start | bytes 1179656 | tf_op jit(solution)/shard_map/ppermute | solution.py:22
  121.2 19.0 %collective-permute-start.34 = (f32[256,512]{1,0:T(8,128)S(1)}, f32[256,512]{1,0:T(8,128)S(1)}, u32[]{:S(2)}, u32[]{:S(2)}) collective-permute-start(f32[256,512]{1,0:T(8,128)S(1)} %get-tuple-element.81.h3_ref), channel_id=1, source_target_pairs={{0,16},{16,32},{32,48},{48,64},{64,80},{80,96},{96,112},{112,0},{1... | collective-permute-start | bytes 1572872 | tf_op jit(solution)/shard_map/ppermute | solution.py:18
  121.2 19.0 %collective-permute-start.35 = (f32[256,512]{1,0:T(8,128)S(1)}, f32[256,512]{1,0:T(8,128)S(1)}, u32[]{:S(2)}, u32[]{:S(2)}) collective-permute-start(f32[256,512]{1,0:T(8,128)S(1)} %get-tuple-element.72.h0_ref), channel_id=1, source_target_pairs={{0,112},{16,0},{32,16},{48,32},{64,48},{80,64},{96,80},{112,96},{1... | collective-permute-start | bytes 1572872 | tf_op jit(solution)/shard_map/ppermute | solution.py:18
  128.8 17.6 %collective-permute-start.25 = (f32[256,512]{1,0:T(8,128)S(1)}, f32[256,512]{1,0:T(8,128)S(1)}, u32[]{:S(2)}, u32[]{:S(2)}) collective-permute-start(f32[256,512]{1,0:T(8,128)S(1)} %get-tuple-element.76.h3_ref), channel_id=1, source_target_pairs={{0,16},{16,32},{32,48},{48,64},{64,80},{80,96},{96,112},{112,0},{1... | collective-permute-start | bytes 1572872 | tf_op jit(solution)/shard_map/ppermute | solution.py:18
  128.9 17.5 %collective-permute-start.26 = (f32[256,512]{1,0:T(8,128)S(1)}, f32[256,512]{1,0:T(8,128)S(1)}, u32[]{:S(2)}, u32[]{:S(2)}) collective-permute-start(f32[256,512]{1,0:T(8,128)S(1)} %get-tuple-element.77.h0_ref), channel_id=1, source_target_pairs={{0,112},{16,0},{32,16},{48,32},{64,48},{80,64},{96,80},{112,96},{1... | collective-permute-start | bytes 1572872 | tf_op jit(solution)/shard_map/ppermute | solution.py:18
  133.0 1.7 %collective-permute-start.33 = (f32[2,3,32,512]{3,2,1,0:T(8,128)S(1)}, f32[2,3,32,512]{3,2,1,0:T(8,128)S(1)}, u32[]{:S(2)}, u32[]{:S(2)}) collective-permute-start(f32[2,3,32,512]{3,2,1,0:T(8,128)S(1)} %collective-permute-done.29.refs_3_), channel_id=1, source_target_pairs={{0,1},{1,0},{2,3},{3,2},{4,5},{5,4},{6,7},{7,6},{8,9},{9,8},{10,11... | collective-permute-start | bytes 1179656 | tf_op jit(solution)/shard_map/ppermute | solution.py:22

commit v2 on v1

--- a/solution.py
+++ b/solution.py
@@ -293,7 +293,7 @@
         order = after(order, halos[c - 2]) if c > 1 else order
         strips[c] = rounds12(a, *strips[c], f, order, lo12)
         halos[c] = exchanged(strips[c])
-    late = both_cores(list(after(late, strips[1])))
+    late = both_cores(list(after(late, strips[0][0])))
     owners = jnp.concatenate([owner_table[3], next_owner[3:]], 0)
     hi3, lo3 = prep(late, placement, owners, "place3")
     result = None

time: 150 us -> 171 us (1.14)
  waiting for transfers between devices: 55.5 us -> 76.8 us
    ppermute x13, waiting for transfers between devices: 9.91 us -> 32.2 us  [shifted(): lax.ppermute(value, 'sec', [(i, (i + steps) % count) for i in range(count)])]
  transfers between devices with their start and end apart: 36 -> 36, of which waited for: 13 -> 13; matrix products, arithmetic and copies ran while one was open for 2% -> 2% of each run, Pallas kernels for 24% -> 21%
where the time goes in v2:
time: 171 us
  waiting for transfers between devices  76.8 us (45%)
  starting transfers between devices  50.9 us (30%)
  Pallas kernels  38.2 us (22%)
  local copies, waits for them, and re-layouts  3.95 us (2%)
    ppermute x23, waiting for transfers between devices, moved(): return lax.ppermute(value, 'col', [(i, target(i)) for i in range(16)])  44.6 us
    pallas_call x12, Pallas kernels, kernel(): pl.pallas_call(body, in_specs=in_specs, out_specs=out_specs, out_shape=ou...  38.2 us
    ppermute x13, waiting for transfers between devices, shifted(): lax.ppermute(value, 'sec', [(i, (i + steps) % count) for i in range(count)])  32.2 us
    ppermute x13, starting transfers between devices, shifted(): lax.ppermute(value, 'sec', [(i, (i + steps) % count) for i in range(count)])  27.8 us
    ppermute x23, starting transfers between devices, moved(): return lax.ppermute(value, 'col', [(i, target(i)) for i in range(16)])  23.1 us
  transfers between devices with their start and end apart: 36, of which 13 were waited for; matrix products, arithmetic and copies ran while one was open for 2% of the time, Pallas kernels for 21%

profile of v2, /device:TPU:0, one launch (start us, length us, event | category | flops | bytes accessed | tf_op | source)
XLA Modules:
  0.0 170.5 jit_solution(8739245040391420151)
XLA Ops:
  0.0 1.2 slice_bitcast_fusion.3
  1.2 3.2 %collective-permute-start = (f32[2,32,512]{2,1,0:T(8,128)S(1)}, f32[2,32,512]{2,1,0:T(8,128)S(1)}, u32[]{:S(2)}, u32[]{:S(2)}) collective-permute-start(f32[2,32,512]{2,1,0:T(8,128)S(1)} %get-tuple-element.90), channel_id=1, source_target_pairs={{0,8},{1,9},{2,10},{3,11},{4,12},{5,13},{6,14},{7,15},{8,0},{9,1},... | collective-permute-start | bytes 393224 | tf_op jit(solution)/shard_map/ppermute | solution.py:22
  4.4 1.0 slice.106
  5.4 0.8 bitcast_dynamic-update-slice_fusion.1
  6.2 1.6 collective-permute-done
  7.9 4.2 %collective-permute-start.3 = (f32[2,2,32,512]{3,2,1,0:T(8,128)S(1)}, f32[2,2,32,512]{3,2,1,0:T(8,128)S(1)}, u32[]{:S(2)}, u32[]{:S(2)}) collective-permute-start(f32[2,2,32,512]{3,2,1,0:T(8,128)S(1)} %pad_maximum_fusion.2.refs_0_), channel_id=1, source_target_pairs={{0,4},{1,5},{2,6},{3,7},{4,0},{5,1},{6,2},{7,3},{8,12},{9,13},{10,... | collective-permute-start | bytes 786440 | tf_op jit(solution)/shard_map/ppermute | solution.py:22
  12.1 0.7 collective-permute-start.2
  12.8 1.3 collective-permute-start.1
  14.1 3.0 %collective-permute-start.12 = (f32[3,2,32,512]{3,2,1,0:T(8,128)S(1)}, f32[3,2,32,512]{3,2,1,0:T(8,128)S(1)}, u32[]{:S(2)}, u32[]{:S(2)}) collective-permute-start(f32[3,2,32,512]{3,2,1,0:T(8,128)S(1)} %slice.106), channel_id=1, source_target_pairs={{0,8},{1,9},{2,10},{3,11},{4,12},{5,13},{6,14},{7,15},{8,0},{9,1},... | collective-permute-start | bytes 1179656 | tf_op jit(solution)/shard_map/ppermute | solution.py:22
  17.1 0.8 bitcast_dynamic-update-slice_fusion
  18.0 1.3 collective-permute-done.3.refs_3_
  19.3 4.6 %collective-permute-done.2.refs_2_ = f32[2,2,32,512]{3,2,1,0:T(8,128)S(1)} collective-permute-done((f32[2,2,32,512]{3,2,1,0:T(8,128)S(1)}, f32[2,2,32,512]{3,2,1,0:T(8,128)S(1)}, u32[]{:S(2)}, u32[]{:S(2)}) %collective-permute-start.2) | collective-permute-done | bytes 262176 | tf_op jit(solution)/shard_map/ppermute | solution.py:22
  23.9 0.5 collective-permute-start.5
  24.8 4.0 %collective-permute-start.13 = (f32[136,512]{1,0:T(8,128)S(1)}, f32[136,512]{1,0:T(8,128)S(1)}, u32[]{:S(2)}, u32[]{:S(2)}) collective-permute-start(f32[136,512]{1,0:T(8,128)S(1)} %pad_dynamic-update-slice_fusion), channel_id=1, source_target_pairs={{0,112},{16,0},{32,16},{48,32},{64,48},{80,64},{96,80},{112,96},{1... | collective-permute-start | bytes 835592 | tf_op jit(solution)/shard_map/ppermute | solution.py:18
  28.8 0.9 place0.1
  29.7 5.2 %round0.3 = (f32[256,1024]{1,0:T(8,128)S(1)}, f32[512,1024]{1,0:T(8,128)S(1)}, f32[256,1024]{1,0:T(8,128)S(1)}) custom-call(f32[1024,2048]{1,0:T(8,128)} %x_ref.5, bf16[2,512,512]{2,1,0:T(8,128)(2,1)S(1)} %get-tuple-element.54.hi_ref, bf16[2,512,512]{2,1,0:T(8,128)(2,1)S(1)} %get-tuple-element.48.lo_ref), custom_call_target="tpu_custom_call" | custom-call | flops 32212254 | bytes 20971 | tf_op jit(solution)/shard_map/round0/pallas_call | solution.py:38
  35.0 4.1 %collective-permute-start.9 = (f32[256,1024]{1,0:T(8,128)S(1)}, f32[256,1024]{1,0:T(8,128)S(1)}, u32[]{:S(2)}, u32[]{:S(2)}) collective-permute-start(f32[256,1024]{1,0:T(8,128)S(1)} %get-tuple-element.49.h0_ref), channel_id=1, source_target_pairs={{0,112},{16,0},{32,16},{48,32},{64,48},{80,64},{96,80},{112,96},{1... | collective-permute-start | bytes 3145736 | tf_op jit(solution)/shard_map/ppermute | solution.py:18
  39.3 1.7 %collective-permute-start.16 = (f32[2,5,32,512]{3,2,1,0:T(8,128)S(1)}, f32[2,5,32,512]{3,2,1,0:T(8,128)S(1)}, u32[]{:S(2)}, u32[]{:S(2)}) collective-permute-start(f32[2,5,32,512]{3,2,1,0:T(8,128)S(1)} %pad_maximum_fusion.refs_0_), channel_id=1, source_target_pairs={{0,4},{1,5},{2,6},{3,7},{4,0},{5,1},{6,2},{7,3},{8,12},{9,13},{10,... | collective-permute-start | bytes 1966088 | tf_op jit(solution)/shard_map/ppermute | solution.py:22
  41.0 2.0 %collective-permute-start.15 = (f32[2,5,32,512]{3,2,1,0:T(8,128)S(1)}, f32[2,5,32,512]{3,2,1,0:T(8,128)S(1)}, u32[]{:S(2)}, u32[]{:S(2)}) collective-permute-start(f32[2,5,32,512]{3,2,1,0:T(8,128)S(1)} %pad_maximum_fusion.refs_0_), channel_id=1, source_target_pairs={{0,6},{1,7},{2,0},{3,1},{4,2},{5,3},{6,4},{7,5},{8,14},{9,15},{10,... | collective-permute-start | bytes 1966088 | tf_op jit(solution)/shard_map/ppermute | solution.py:22
  43.1 3.2 %round0.4 = (f32[256,512]{1,0:T(8,128)S(1)}, f32[512,512]{1,0:T(8,128)S(1)}, f32[256,512]{1,0:T(8,128)S(1)}) custom-call(f32[1024,2048]{1,0:T(8,128)} %x_ref.5, bf16[2,512,512]{2,1,0:T(8,128)(2,1)S(1)} %get-tuple-element.54.hi_ref, bf16[2,512,512]{2,1,0:T(8,128)(2,1)S(1)} %get-tuple-element.48.lo_ref), custom_call_target="tpu_custom_call" | custom-call | flops 16106127 | bytes 20971 | tf_op jit(solution)/shard_map/round0/pallas_call | solution.py:38
  46.3 12.3 %collective-permute-done.16.refs_3_ = f32[2,5,32,512]{3,2,1,0:T(8,128)S(1)} collective-permute-done((f32[2,5,32,512]{3,2,1,0:T(8,128)S(1)}, f32[2,5,32,512]{3,2,1,0:T(8,128)S(1)}, u32[]{:S(2)}, u32[]{:S(2)}) %collective-permute-start.16) | collective-permute-done | bytes 655392 | tf_op jit(solution)/shard_map/ppermute | solution.py:22
  58.6 11.8 %collective-permute-done.15.refs_2_ = f32[2,5,32,512]{3,2,1,0:T(8,128)S(1)} collective-permute-done((f32[2,5,32,512]{3,2,1,0:T(8,128)S(1)}, f32[2,5,32,512]{3,2,1,0:T(8,128)S(1)}, u32[]{:S(2)}, u32[]{:S(2)}) %collective-permute-start.15) | collective-permute-done | bytes 655392 | tf_op jit(solution)/shard_map/ppermute | solution.py:22
  71.1 0.5 collective-permute-start.20
  71.6 0.9 collective-permute-done.17.refs_4_
  72.6 3.0 %collective-permute-start.22 = (f32[256,512]{1,0:T(8,128)S(1)}, f32[256,512]{1,0:T(8,128)S(1)}, u32[]{:S(2)}, u32[]{:S(2)}) collective-permute-start(f32[256,512]{1,0:T(8,128)S(1)} %get-tuple-element.51.h0_ref), channel_id=1, source_target_pairs={{0,112},{16,0},{32,16},{48,32},{64,48},{80,64},{96,80},{112,96},{1... | collective-permute-start | bytes 1572872 | tf_op jit(solution)/shard_map/ppermute | solution.py:18
  75.6 2.4 %collective-permute-start.29 = (f32[2,3,32,512]{3,2,1,0:T(8,128)S(1)}, f32[2,3,32,512]{3,2,1,0:T(8,128)S(1)}, u32[]{:S(2)}, u32[]{:S(2)}) collective-permute-start(f32[2,3,32,512]{3,2,1,0:T(8,128)S(1)} %pad_maximum_fusion.1.refs_0_), channel_id=1, source_target_pairs={{0,4},{1,5},{2,6},{3,7},{4,0},{5,1},{6,2},{7,3},{8,12},{9,13},{10,... | collective-permute-start | bytes 1179656 | tf_op jit(solution)/shard_map/ppermute | solution.py:22
  78.0 1.3 collective-permute-start.28
  79.3 1.3 place12.1
  80.6 6.8 %collective-permute-done.21.a_ref = f32[256,512]{1,0:T(8,128)S(1)} collective-permute-done((f32[256,512]{1,0:T(8,128)S(1)}, f32[256,512]{1,0:T(8,128)S(1)}, u32[]{:S(2)}, u32[]{:S(2)}) %collective-permute-start.21) | collective-permute-done | bytes 524320 | tf_op jit(solution)/shard_map/ppermute | solution.py:18
  87.4 6.7 %rounds12.3 = (f32[256,1024]{1,0:T(8,128)S(1)}, f32[512,1024]{1,0:T(8,128)S(1)}, f32[256,1024]{1,0:T(8,128)S(1)}) custom-call(f32[256,1024]{1,0:T(8,128)S(1)} %collective-permute-done.8.a_ref, f32[256,1024]{1,0:T(8,128)S(1)} %get-tuple-element.49.h0_ref, f32[512,1024]{1,0:T(8,128)S(1)} %get-tuple-element.67.h12_ref, ...), custom_call_target="tpu_custom_call" | custom-call | flops 64424508 | bytes 115343 | tf_op jit(solution)/shard_map/rounds12/pallas_call | solution.py:38
  94.2 4.5 %collective-permute-start.24 = (f32[256,1024]{1,0:T(8,128)S(1)}, f32[256,1024]{1,0:T(8,128)S(1)}, u32[]{:S(2)}, u32[]{:S(2)}) collective-permute-start(f32[256,1024]{1,0:T(8,128)S(1)} %get-tuple-element.70.h0_ref), channel_id=1, source_target_pairs={{0,112},{16,0},{32,16},{48,32},{64,48},{80,64},{96,80},{112,96},{1... | collective-permute-start | bytes 3145736 | tf_op jit(solution)/shard_map/ppermute | solution.py:18
  98.7 3.2 %round0.5 = (f32[256,512]{1,0:T(8,128)S(1)}, f32[512,512]{1,0:T(8,128)S(1)}, f32[256,512]{1,0:T(8,128)S(1)}) custom-call(f32[1024,2048]{1,0:T(8,128)} %x_ref.5, bf16[2,512,512]{2,1,0:T(8,128)(2,1)S(1)} %get-tuple-element.54.hi_ref, bf16[2,512,512]{2,1,0:T(8,128)(2,1)S(1)} %get-tuple-element.48.lo_ref), custom_call_target="tpu_custom_call" | custom-call | flops 16106127 | bytes 20971 | tf_op jit(solution)/shard_map/round0/pallas_call | solution.py:38
  102.0 4.1 %collective-permute-start.11 = (f32[256,512]{1,0:T(8,128)S(1)}, f32[256,512]{1,0:T(8,128)S(1)}, u32[]{:S(2)}, u32[]{:S(2)}) collective-permute-start(f32[256,512]{1,0:T(8,128)S(1)} %get-tuple-element.56.h0_ref), channel_id=1, source_target_pairs={{0,112},{16,0},{32,16},{48,32},{64,48},{80,64},{96,80},{112,96},{1... | collective-permute-start | bytes 1572872 | tf_op jit(solution)/shard_map/ppermute | solution.py:18
  106.2 1.0 collective-permute-start.27
  107.2 9.9 %collective-permute-done.27.refs_1_ = f32[2,3,32,512]{3,2,1,0:T(8,128)S(1)} collective-permute-done((f32[2,3,32,512]{3,2,1,0:T(8,128)S(1)}, f32[2,3,32,512]{3,2,1,0:T(8,128)S(1)}, u32[]{:S(2)}, u32[]{:S(2)}) %collective-permute-start.27) | collective-permute-done | bytes 393248 | tf_op jit(solution)/shard_map/ppermute | solution.py:22
  117.1 15.7 %collective-permute-done.10.a_ref = f32[256,512]{1,0:T(8,128)S(1)} collective-permute-done((f32[256,512]{1,0:T(8,128)S(1)}, f32[256,512]{1,0:T(8,128)S(1)}, u32[]{:S(2)}, u32[]{:S(2)}) %collective-permute-start.10) | collective-permute-done | bytes 524320 | tf_op jit(solution)/shard_map/ppermute | solution.py:18
  132.8 0.5 collective-permute-start.32
  133.3 3.4 %rounds12.4 = (f32[256,512]{1,0:T(8,128)S(1)}, f32[512,512]{1,0:T(8,128)S(1)}, f32[256,512]{1,0:T(8,128)S(1)}) custom-call(f32[256,512]{1,0:T(8,128)S(1)} %collective-permute-done.21.a_ref, f32[256,512]{1,0:T(8,128)S(1)} %get-tuple-element.51.h0_ref, f32[512,512]{1,0:T(8,128)S(1)} %get-tuple-element.60.h12_ref, f32[256,512]{1,0:T(8,128)S(1)} %get-tuple-element.61.h3_ref, ...), custom_call_target="tpu_custom_call" | custom-call | flops 32212254 | bytes 83886 | tf_op jit(solution)/shard_map/rounds12/pallas_call | solution.py:38
  136.7 3.5 %collective-permute-start.35 = (f32[256,512]{1,0:T(8,128)S(1)}, f32[256,512]{1,0:T(8,128)S(1)}, u32[]{:S(2)}, u32[]{:S(2)}) collective-permute-start(f32[256,512]{1,0:T(8,128)S(1)} %get-tuple-element.72.h0_ref), channel_id=1, source_target_pairs={{0,112},{16,0},{32,16},{48,32},{64,48},{80,64},{96,80},{112,96},{1... | collective-permute-start | bytes 1572872 | tf_op jit(solution)/shard_map/ppermute | solution.py:18
  140.2 3.4 %rounds12.5 = (f32[256,512]{1,0:T(8,128)S(1)}, f32[512,512]{1,0:T(8,128)S(1)}, f32[256,512]{1,0:T(8,128)S(1)}) custom-call(f32[256,512]{1,0:T(8,128)S(1)} %collective-permute-done.10.a_ref, f32[256,512]{1,0:T(8,128)S(1)} %get-tuple-element.56.h0_ref, f32[512,512]{1,0:T(8,128)S(1)} %get-tuple-element.57.h12_ref, f32[256,512]{1,0:T(8,128)S(1)} %get-tuple-element.55.h3_ref, ...), custom_call_target="tpu_custom_call" | custom-call | flops 32212254 | bytes 83886 | tf_op jit(solution)/shard_map/rounds12/pallas_call | solution.py:38
  143.7 4.2 %collective-permute-start.26 = (f32[256,512]{1,0:T(8,128)S(1)}, f32[256,512]{1,0:T(8,128)S(1)}, u32[]{:S(2)}, u32[]{:S(2)}) collective-permute-start(f32[256,512]{1,0:T(8,128)S(1)} %get-tuple-element.77.h0_ref), channel_id=1, source_target_pairs={{0,112},{16,0},{32,16},{48,32},{64,48},{80,64},{96,80},{112,96},{1... | collective-permute-start | bytes 1572872 | tf_op jit(solution)/shard_map/ppermute | solution.py:18
  148.0 1.7 %collective-permute-done.33.refs_7_ = f32[2,3,32,512]{3,2,1,0:T(8,128)S(1)} collective-permute-done((f32[2,3,32,512]{3,2,1,0:T(8,128)S(1)}, f32[2,3,32,512]{3,2,1,0:T(8,128)S(1)}, u32[]{:S(2)}, u32[]{:S(2)}) %collective-permute-start.33) | collective-permute-done | bytes 393248 | tf_op jit(solution)/shard_map/ppermute | solution.py:22
  149.7 1.0 place3.1
  150.7 4.5 %round3.3.rest_0_ = f32[1024,2048]{1,0:T(8,128)} custom-call(f32[256,1024]{1,0:T(8,128)S(1)} %collective-permute-done.23.a_ref, f32[256,1024]{1,0:T(8,128)S(1)} %get-tuple-element.70.h0_ref, f32[512,1024]{1,0:T(8,128)S(1)} %get-tuple-element.88.h12_ref, f32[256,1024]{1,0:T(8,128)S(1)} %get-tuple-element.74.h3_ref, ...), custom_call_target="tpu_custom_call" | custom-call | flops 32212254 | bytes 94371 | tf_op jit(solution)/shard_map/round3/pallas_call | solution.py:38
  155.2 1.9 %collective-permute-done.34.a_ref = f32[256,512]{1,0:T(8,128)S(1)} collective-permute-done((f32[256,512]{1,0:T(8,128)S(1)}, f32[256,512]{1,0:T(8,128)S(1)}, u32[]{:S(2)}, u32[]{:S(2)}) %collective-permute-start.34) | collective-permute-done | bytes 524320 | tf_op jit(solution)/shard_map/ppermute | solution.py:18
  157.1 2.7 %round3.4.rest_0_ = f32[1024,2048]{1,0:T(8,128)} custom-call(f32[256,512]{1,0:T(8,128)S(1)} %collective-permute-done.34.a_ref, f32[256,512]{1,0:T(8,128)S(1)} %get-tuple-element.72.h0_ref, f32[512,512]{1,0:T(8,128)S(1)} %get-tuple-element.87.h12_ref, f32[256,512]{1,0:T(8,128)S(1)} %get-tuple-element.86.h3_ref, ...), custom_call_target="tpu_custom_call", output_to_operand_aliasing={{}: (7, {})} | custom-call | flops 16106127 | bytes 62914 | tf_op jit(solution)/shard_map/round3/pallas_call | solution.py:38
  159.8 7.8 %collective-permute-done.25.a_ref = f32[256,512]{1,0:T(8,128)S(1)} collective-permute-done((f32[256,512]{1,0:T(8,128)S(1)}, f32[256,512]{1,0:T(8,128)S(1)}, u32[]{:S(2)}, u32[]{:S(2)}) %collective-permute-start.25) | collective-permute-done | bytes 524320 | tf_op jit(solution)/shard_map/ppermute | solution.py:18
  167.6 2.7 %round3.5 = f32[1024,2048]{1,0:T(8,128)} custom-call(f32[256,512]{1,0:T(8,128)S(1)} %collective-permute-done.25.a_ref, f32[256,512]{1,0:T(8,128)S(1)} %get-tuple-element.77.h0_ref, f32[512,512]{1,0:T(8,128)S(1)} %get-tuple-element.78.h12_ref, f32[256,512]{1,0:T(8,128)S(1)} %get-tuple-element.76.h3_ref, ...), custom_call_target="tpu_custom_call", output_to_operand_aliasing={{}: (7, {})} | custom-call | flops 16106127 | bytes 62914 | tf_op jit(solution)/shard_map/round3/pallas_call | solution.py:38
  (60 shorter events, 1.7 us)
Async XLA Ops:
  0.0 17.1 %copy-start = (s32[4,2,16]{2,1,0:T(2,128)S(1)}, s32[4,2,16]{2,1,0:T(2,128)}, u32[]{:S(2)}) copy-start(s32[4,2,16]{2,1,0:T(2,128)} %param.5) | copy-start | bytes 1540
  1.2 6.7 %collective-permute-start = (f32[2,32,512]{2,1,0:T(8,128)S(1)}, f32[2,32,512]{2,1,0:T(8,128)S(1)}, u32[]{:S(2)}, u32[]{:S(2)}) collective-permute-start(f32[2,32,512]{2,1,0:T(8,128)S(1)} %get-tuple-element.90), channel_id=1, source_target_pairs={{0,8},{1,9},{2,10},{3,11},{4,12},{5,13},{6,14},{7,15},{8,0},{9,1},... | collective-permute-start | bytes 393224 | tf_op jit(solution)/shard_map/ppermute | solution.py:22
  7.9 11.4 %collective-permute-start.3 = (f32[2,2,32,512]{3,2,1,0:T(8,128)S(1)}, f32[2,2,32,512]{3,2,1,0:T(8,128)S(1)}, u32[]{:S(2)}, u32[]{:S(2)}) collective-permute-start(f32[2,2,32,512]{3,2,1,0:T(8,128)S(1)} %pad_maximum_fusion.2.refs_0_), channel_id=1, source_target_pairs={{0,4},{1,5},{2,6},{3,7},{4,0},{5,1},{6,2},{7,3},{8,12},{9,13},{10,... | collective-permute-start | bytes 786440 | tf_op jit(solution)/shard_map/ppermute | solution.py:22
  12.1 11.8 %collective-permute-start.2 = (f32[2,2,32,512]{3,2,1,0:T(8,128)S(1)}, f32[2,2,32,512]{3,2,1,0:T(8,128)S(1)}, u32[]{:S(2)}, u32[]{:S(2)}) collective-permute-start(f32[2,2,32,512]{3,2,1,0:T(8,128)S(1)} %pad_maximum_fusion.2.refs_0_), channel_id=1, source_target_pairs={{0,6},{1,7},{2,0},{3,1},{4,2},{5,3},{6,4},{7,5},{8,14},{9,15},{10,... | collective-permute-start | bytes 786440 | tf_op jit(solution)/shard_map/ppermute | solution.py:22
  12.8 11.1 %collective-permute-start.1 = (f32[2,2,32,512]{3,2,1,0:T(8,128)S(1)}, f32[2,2,32,512]{3,2,1,0:T(8,128)S(1)}, u32[]{:S(2)}, u32[]{:S(2)}) collective-permute-start(f32[2,2,32,512]{3,2,1,0:T(8,128)S(1)} %pad_maximum_fusion.2.refs_0_), channel_id=1, source_target_pairs={{0,2},{1,3},{2,4},{3,5},{4,6},{5,7},{6,0},{7,1},{8,10},{9,11},{10,... | collective-permute-start | bytes 786440 | tf_op jit(solution)/shard_map/ppermute | solution.py:22
  14.1 10.6 %collective-permute-start.12 = (f32[3,2,32,512]{3,2,1,0:T(8,128)S(1)}, f32[3,2,32,512]{3,2,1,0:T(8,128)S(1)}, u32[]{:S(2)}, u32[]{:S(2)}) collective-permute-start(f32[3,2,32,512]{3,2,1,0:T(8,128)S(1)} %slice.106), channel_id=1, source_target_pairs={{0,8},{1,9},{2,10},{3,11},{4,12},{5,13},{6,14},{7,15},{8,0},{9,1},... | collective-permute-start | bytes 1179656 | tf_op jit(solution)/shard_map/ppermute | solution.py:22
  18.0 10.9 %collective-permute-start.4 = (f32[2,2,32,512]{3,2,1,0:T(8,128)S(1)}, f32[2,2,32,512]{3,2,1,0:T(8,128)S(1)}, u32[]{:S(2)}, u32[]{:S(2)}) collective-permute-start(f32[2,2,32,512]{3,2,1,0:T(8,128)S(1)} %pad_maximum_fusion.2.refs_0_), channel_id=1, source_target_pairs={{0,1},{1,0},{2,3},{3,2},{4,5},{5,4},{6,7},{7,6},{8,9},{9,8},{10,11... | collective-permute-start | bytes 786440 | tf_op jit(solution)/shard_map/ppermute | solution.py:22
  19.3 9.5 %collective-permute-start.7 = (f32[2,2,32,512]{3,2,1,0:T(8,128)S(1)}, f32[2,2,32,512]{3,2,1,0:T(8,128)S(1)}, u32[]{:S(2)}, u32[]{:S(2)}) collective-permute-start(f32[2,2,32,512]{3,2,1,0:T(8,128)S(1)} %collective-permute-done.3.refs_3_), channel_id=1, source_target_pairs={{0,1},{1,0},{2,3},{3,2},{4,5},{5,4},{6,7},{7,6},{8,9},{9,8},{10,11... | collective-permute-start | bytes 786440 | tf_op jit(solution)/shard_map/ppermute | solution.py:22
  23.9 4.9 %collective-permute-start.6 = (f32[2,2,32,512]{3,2,1,0:T(8,128)S(1)}, f32[2,2,32,512]{3,2,1,0:T(8,128)S(1)}, u32[]{:S(2)}, u32[]{:S(2)}) collective-permute-start(f32[2,2,32,512]{3,2,1,0:T(8,128)S(1)} %collective-permute-done.2.refs_2_), channel_id=1, source_target_pairs={{0,1},{1,0},{2,3},{3,2},{4,5},{5,4},{6,7},{7,6},{8,9},{9,8},{10,11... | collective-permute-start | bytes 786440 | tf_op jit(solution)/shard_map/ppermute | solution.py:22
  23.9 5.0 %collective-permute-start.5 = (f32[2,2,32,512]{3,2,1,0:T(8,128)S(1)}, f32[2,2,32,512]{3,2,1,0:T(8,128)S(1)}, u32[]{:S(2)}, u32[]{:S(2)}) collective-permute-start(f32[2,2,32,512]{3,2,1,0:T(8,128)S(1)} %collective-permute-done.1.refs_1_), channel_id=1, source_target_pairs={{0,1},{1,0},{2,3},{3,2},{4,5},{5,4},{6,7},{7,6},{8,9},{9,8},{10,11... | collective-permute-start | bytes 786440 | tf_op jit(solution)/shard_map/ppermute | solution.py:22
  24.8 14.4 %collective-permute-start.13 = (f32[136,512]{1,0:T(8,128)S(1)}, f32[136,512]{1,0:T(8,128)S(1)}, u32[]{:S(2)}, u32[]{:S(2)}) collective-permute-start(f32[136,512]{1,0:T(8,128)S(1)} %pad_dynamic-update-slice_fusion), channel_id=1, source_target_pairs={{0,112},{16,0},{32,16},{48,32},{64,48},{80,64},{96,80},{112,96},{1... | collective-permute-start | bytes 835592 | tf_op jit(solution)/shard_map/ppermute | solution.py:18
  34.9 35.5 %collective-permute-start.8 = (f32[256,1024]{1,0:T(8,128)S(1)}, f32[256,1024]{1,0:T(8,128)S(1)}, u32[]{:S(2)}, u32[]{:S(2)}) collective-permute-start(f32[256,1024]{1,0:T(8,128)S(1)} %get-tuple-element.53.h3_ref), channel_id=1, source_target_pairs={{0,16},{16,32},{32,48},{48,64},{64,80},{80,96},{96,112},{112,0},{1... | collective-permute-start | bytes 3145736 | tf_op jit(solution)/shard_map/ppermute | solution.py:18
  35.0 35.4 %collective-permute-start.9 = (f32[256,1024]{1,0:T(8,128)S(1)}, f32[256,1024]{1,0:T(8,128)S(1)}, u32[]{:S(2)}, u32[]{:S(2)}) collective-permute-start(f32[256,1024]{1,0:T(8,128)S(1)} %get-tuple-element.49.h0_ref), channel_id=1, source_target_pairs={{0,112},{16,0},{32,16},{48,32},{64,48},{80,64},{96,80},{112,96},{1... | collective-permute-start | bytes 3145736 | tf_op jit(solution)/shard_map/ppermute | solution.py:18
  39.3 19.3 %collective-permute-start.16 = (f32[2,5,32,512]{3,2,1,0:T(8,128)S(1)}, f32[2,5,32,512]{3,2,1,0:T(8,128)S(1)}, u32[]{:S(2)}, u32[]{:S(2)}) collective-permute-start(f32[2,5,32,512]{3,2,1,0:T(8,128)S(1)} %pad_maximum_fusion.refs_0_), channel_id=1, source_target_pairs={{0,4},{1,5},{2,6},{3,7},{4,0},{5,1},{6,2},{7,3},{8,12},{9,13},{10,... | collective-permute-start | bytes 1966088 | tf_op jit(solution)/shard_map/ppermute | solution.py:22
  41.0 29.4 %collective-permute-start.15 = (f32[2,5,32,512]{3,2,1,0:T(8,128)S(1)}, f32[2,5,32,512]{3,2,1,0:T(8,128)S(1)}, u32[]{:S(2)}, u32[]{:S(2)}) collective-permute-start(f32[2,5,32,512]{3,2,1,0:T(8,128)S(1)} %pad_maximum_fusion.refs_0_), channel_id=1, source_target_pairs={{0,6},{1,7},{2,0},{3,1},{4,2},{5,3},{6,4},{7,5},{8,14},{9,15},{10,... | collective-permute-start | bytes 1966088 | tf_op jit(solution)/shard_map/ppermute | solution.py:22
  43.0 27.3 %collective-permute-start.14 = (f32[2,5,32,512]{3,2,1,0:T(8,128)S(1)}, f32[2,5,32,512]{3,2,1,0:T(8,128)S(1)}, u32[]{:S(2)}, u32[]{:S(2)}) collective-permute-start(f32[2,5,32,512]{3,2,1,0:T(8,128)S(1)} %pad_maximum_fusion.refs_0_), channel_id=1, source_target_pairs={{0,2},{1,3},{2,4},{3,5},{4,6},{5,7},{6,0},{7,1},{8,10},{9,11},{10,... | collective-permute-start | bytes 1966088 | tf_op jit(solution)/shard_map/ppermute | solution.py:22
  70.4 2.2 %collective-permute-start.17 = (f32[2,5,32,512]{3,2,1,0:T(8,128)S(1)}, f32[2,5,32,512]{3,2,1,0:T(8,128)S(1)}, u32[]{:S(2)}, u32[]{:S(2)}) collective-permute-start(f32[2,5,32,512]{3,2,1,0:T(8,128)S(1)} %pad_maximum_fusion.refs_0_), channel_id=1, source_target_pairs={{0,1},{1,0},{2,3},{3,2},{4,5},{5,4},{6,7},{7,6},{8,9},{9,8},{10,11... | collective-permute-start | bytes 1966088 | tf_op jit(solution)/shard_map/ppermute | solution.py:22
  70.5 5.1 %collective-permute-start.18 = (f32[2,5,32,512]{3,2,1,0:T(8,128)S(1)}, f32[2,5,32,512]{3,2,1,0:T(8,128)S(1)}, u32[]{:S(2)}, u32[]{:S(2)}) collective-permute-start(f32[2,5,32,512]{3,2,1,0:T(8,128)S(1)} %collective-permute-done.14.refs_1_), channel_id=1, source_target_pairs={{0,1},{1,0},{2,3},{3,2},{4,5},{5,4},{6,7},{7,6},{8,9},{9,8},{10,11... | collective-permute-start | bytes 1966088 | tf_op jit(solution)/shard_map/ppermute | solution.py:22
  71.0 7.0 %collective-permute-start.19 = (f32[2,5,32,512]{3,2,1,0:T(8,128)S(1)}, f32[2,5,32,512]{3,2,1,0:T(8,128)S(1)}, u32[]{:S(2)}, u32[]{:S(2)}) collective-permute-start(f32[2,5,32,512]{3,2,1,0:T(8,128)S(1)} %collective-permute-done.15.refs_2_), channel_id=1, source_target_pairs={{0,1},{1,0},{2,3},{3,2},{4,5},{5,4},{6,7},{7,6},{8,9},{9,8},{10,11... | collective-permute-start | bytes 1966088 | tf_op jit(solution)/shard_map/ppermute | solution.py:22
  71.1 16.4 %collective-permute-start.21 = (f32[256,512]{1,0:T(8,128)S(1)}, f32[256,512]{1,0:T(8,128)S(1)}, u32[]{:S(2)}, u32[]{:S(2)}) collective-permute-start(f32[256,512]{1,0:T(8,128)S(1)} %get-tuple-element.61.h3_ref), channel_id=1, source_target_pairs={{0,16},{16,32},{32,48},{48,64},{64,80},{80,96},{96,112},{112,0},{1... | collective-permute-start | bytes 1572872 | tf_op jit(solution)/shard_map/ppermute | solution.py:18
  71.1 8.2 %collective-permute-start.20 = (f32[2,5,32,512]{3,2,1,0:T(8,128)S(1)}, f32[2,5,32,512]{3,2,1,0:T(8,128)S(1)}, u32[]{:S(2)}, u32[]{:S(2)}) collective-permute-start(f32[2,5,32,512]{3,2,1,0:T(8,128)S(1)} %collective-permute-done.16.refs_3_), channel_id=1, source_target_pairs={{0,1},{1,0},{2,3},{3,2},{4,5},{5,4},{6,7},{7,6},{8,9},{9,8},{10,11... | collective-permute-start | bytes 1966088 | tf_op jit(solution)/shard_map/ppermute | solution.py:22
  72.6 14.9 %collective-permute-start.22 = (f32[256,512]{1,0:T(8,128)S(1)}, f32[256,512]{1,0:T(8,128)S(1)}, u32[]{:S(2)}, u32[]{:S(2)}) collective-permute-start(f32[256,512]{1,0:T(8,128)S(1)} %get-tuple-element.51.h0_ref), channel_id=1, source_target_pairs={{0,112},{16,0},{32,16},{48,32},{64,48},{80,64},{96,80},{112,96},{1... | collective-permute-start | bytes 1572872 | tf_op jit(solution)/shard_map/ppermute | solution.py:18
  75.6 26.4 %collective-permute-start.29 = (f32[2,3,32,512]{3,2,1,0:T(8,128)S(1)}, f32[2,3,32,512]{3,2,1,0:T(8,128)S(1)}, u32[]{:S(2)}, u32[]{:S(2)}) collective-permute-start(f32[2,3,32,512]{3,2,1,0:T(8,128)S(1)} %pad_maximum_fusion.1.refs_0_), channel_id=1, source_target_pairs={{0,4},{1,5},{2,6},{3,7},{4,0},{5,1},{6,2},{7,3},{8,12},{9,13},{10,... | collective-permute-start | bytes 1179656 | tf_op jit(solution)/shard_map/ppermute | solution.py:22
  78.0 28.2 %collective-permute-start.28 = (f32[2,3,32,512]{3,2,1,0:T(8,128)S(1)}, f32[2,3,32,512]{3,2,1,0:T(8,128)S(1)}, u32[]{:S(2)}, u32[]{:S(2)}) collective-permute-start(f32[2,3,32,512]{3,2,1,0:T(8,128)S(1)} %pad_maximum_fusion.1.refs_0_), channel_id=1, source_target_pairs={{0,6},{1,7},{2,0},{3,1},{4,2},{5,3},{6,4},{7,5},{8,14},{9,15},{10,... | collective-permute-start | bytes 1179656 | tf_op jit(solution)/shard_map/ppermute | solution.py:22
  94.1 42.6 %collective-permute-start.23 = (f32[256,1024]{1,0:T(8,128)S(1)}, f32[256,1024]{1,0:T(8,128)S(1)}, u32[]{:S(2)}, u32[]{:S(2)}) collective-permute-start(f32[256,1024]{1,0:T(8,128)S(1)} %get-tuple-element.74.h3_ref), channel_id=1, source_target_pairs={{0,16},{16,32},{32,48},{48,64},{64,80},{80,96},{96,112},{112,0},{1... | collective-permute-start | bytes 3145736 | tf_op jit(solution)/shard_map/ppermute | solution.py:18
  94.2 46.0 %collective-permute-start.24 = (f32[256,1024]{1,0:T(8,128)S(1)}, f32[256,1024]{1,0:T(8,128)S(1)}, u32[]{:S(2)}, u32[]{:S(2)}) collective-permute-start(f32[256,1024]{1,0:T(8,128)S(1)} %get-tuple-element.70.h0_ref), channel_id=1, source_target_pairs={{0,112},{16,0},{32,16},{48,32},{64,48},{80,64},{96,80},{112,96},{1... | collective-permute-start | bytes 3145736 | tf_op jit(solution)/shard_map/ppermute | solution.py:18
  101.9 30.8 %collective-permute-start.10 = (f32[256,512]{1,0:T(8,128)S(1)}, f32[256,512]{1,0:T(8,128)S(1)}, u32[]{:S(2)}, u32[]{:S(2)}) collective-permute-start(f32[256,512]{1,0:T(8,128)S(1)} %get-tuple-element.55.h3_ref), channel_id=1, source_target_pairs={{0,16},{16,32},{32,48},{48,64},{64,80},{80,96},{96,112},{112,0},{1... | collective-permute-start | bytes 1572872 | tf_op jit(solution)/shard_map/ppermute | solution.py:18
  102.0 30.7 %collective-permute-start.11 = (f32[256,512]{1,0:T(8,128)S(1)}, f32[256,512]{1,0:T(8,128)S(1)}, u32[]{:S(2)}, u32[]{:S(2)}) collective-permute-start(f32[256,512]{1,0:T(8,128)S(1)} %get-tuple-element.56.h0_ref), channel_id=1, source_target_pairs={{0,112},{16,0},{32,16},{48,32},{64,48},{80,64},{96,80},{112,96},{1... | collective-permute-start | bytes 1572872 | tf_op jit(solution)/shard_map/ppermute | solution.py:18
  106.2 10.9 %collective-permute-start.27 = (f32[2,3,32,512]{3,2,1,0:T(8,128)S(1)}, f32[2,3,32,512]{3,2,1,0:T(8,128)S(1)}, u32[]{:S(2)}, u32[]{:S(2)}) collective-permute-start(f32[2,3,32,512]{3,2,1,0:T(8,128)S(1)} %pad_maximum_fusion.1.refs_0_), channel_id=1, source_target_pairs={{0,2},{1,3},{2,4},{3,5},{4,6},{5,7},{6,0},{7,1},{8,10},{9,11},{10,... | collective-permute-start | bytes 1179656 | tf_op jit(solution)/shard_map/ppermute | solution.py:22
  117.1 26.5 %collective-permute-start.30 = (f32[2,3,32,512]{3,2,1,0:T(8,128)S(1)}, f32[2,3,32,512]{3,2,1,0:T(8,128)S(1)}, u32[]{:S(2)}, u32[]{:S(2)}) collective-permute-start(f32[2,3,32,512]{3,2,1,0:T(8,128)S(1)} %pad_maximum_fusion.1.refs_0_), channel_id=1, source_target_pairs={{0,1},{1,0},{2,3},{3,2},{4,5},{5,4},{6,7},{7,6},{8,9},{9,8},{10,11... | collective-permute-start | bytes 1179656 | tf_op jit(solution)/shard_map/ppermute | solution.py:22
  132.8 11.0 %collective-permute-start.31 = (f32[2,3,32,512]{3,2,1,0:T(8,128)S(1)}, f32[2,3,32,512]{3,2,1,0:T(8,128)S(1)}, u32[]{:S(2)}, u32[]{:S(2)}) collective-permute-start(f32[2,3,32,512]{3,2,1,0:T(8,128)S(1)} %collective-permute-done.27.refs_1_), channel_id=1, source_target_pairs={{0,1},{1,0},{2,3},{3,2},{4,5},{5,4},{6,7},{7,6},{8,9},{9,8},{10,11... | collective-permute-start | bytes 1179656 | tf_op jit(solution)/shard_map/ppermute | solution.py:22
  132.8 15.2 %collective-permute-start.32 = (f32[2,3,32,512]{3,2,1,0:T(8,128)S(1)}, f32[2,3,32,512]{3,2,1,0:T(8,128)S(1)}, u32[]{:S(2)}, u32[]{:S(2)}) collective-permute-start(f32[2,3,32,512]{3,2,1,0:T(8,128)S(1)} %collective-permute-done.28.refs_2_), channel_id=1, source_target_pairs={{0,1},{1,0},{2,3},{3,2},{4,5},{5,4},{6,7},{7,6},{8,9},{9,8},{10,11... | collective-permute-start | bytes 1179656 | tf_op jit(solution)/shard_map/ppermute | solution.py:22
  136.7 20.4 %collective-permute-start.35 = (f32[256,512]{1,0:T(8,128)S(1)}, f32[256,512]{1,0:T(8,128)S(1)}, u32[]{:S(2)}, u32[]{:S(2)}) collective-permute-start(f32[256,512]{1,0:T(8,128)S(1)} %get-tuple-element.72.h0_ref), channel_id=1, source_target_pairs={{0,112},{16,0},{32,16},{48,32},{64,48},{80,64},{96,80},{112,96},{1... | collective-permute-start | bytes 1572872 | tf_op jit(solution)/shard_map/ppermute | solution.py:18
  140.2 16.9 %collective-permute-start.34 = (f32[256,512]{1,0:T(8,128)S(1)}, f32[256,512]{1,0:T(8,128)S(1)}, u32[]{:S(2)}, u32[]{:S(2)}) collective-permute-start(f32[256,512]{1,0:T(8,128)S(1)} %get-tuple-element.86.h3_ref), channel_id=1, source_target_pairs={{0,16},{16,32},{32,48},{48,64},{64,80},{80,96},{96,112},{112,0},{1... | collective-permute-start | bytes 1572872 | tf_op jit(solution)/shard_map/ppermute | solution.py:18
  143.6 24.0 %collective-permute-start.25 = (f32[256,512]{1,0:T(8,128)S(1)}, f32[256,512]{1,0:T(8,128)S(1)}, u32[]{:S(2)}, u32[]{:S(2)}) collective-permute-start(f32[256,512]{1,0:T(8,128)S(1)} %get-tuple-element.76.h3_ref), channel_id=1, source_target_pairs={{0,16},{16,32},{32,48},{48,64},{64,80},{80,96},{96,112},{112,0},{1... | collective-permute-start | bytes 1572872 | tf_op jit(solution)/shard_map/ppermute | solution.py:18
  143.7 23.9 %collective-permute-start.26 = (f32[256,512]{1,0:T(8,128)S(1)}, f32[256,512]{1,0:T(8,128)S(1)}, u32[]{:S(2)}, u32[]{:S(2)}) collective-permute-start(f32[256,512]{1,0:T(8,128)S(1)} %get-tuple-element.77.h0_ref), channel_id=1, source_target_pairs={{0,112},{16,0},{32,16},{48,32},{64,48},{80,64},{96,80},{112,96},{1... | collective-permute-start | bytes 1572872 | tf_op jit(solution)/shard_map/ppermute | solution.py:18
  147.9 1.7 %collective-permute-start.33 = (f32[2,3,32,512]{3,2,1,0:T(8,128)S(1)}, f32[2,3,32,512]{3,2,1,0:T(8,128)S(1)}, u32[]{:S(2)}, u32[]{:S(2)}) collective-permute-start(f32[2,3,32,512]{3,2,1,0:T(8,128)S(1)} %collective-permute-done.29.refs_3_), channel_id=1, source_target_pairs={{0,1},{1,0},{2,3},{3,2},{4,5},{5,4},{6,7},{7,6},{8,9},{9,8},{10,11... | collective-permute-start | bytes 1179656 | tf_op jit(solution)/shard_map/ppermute | solution.py:22
